TPU v7x, 128 devices: a whole 4x4x4 slice. The times are simulated.
128 devices in a mesh: ctx: 16 (over z, y_lo, core), head: 8 (over x, y_hi).
Axes of the slice: x: 4, y: 4 (y_hi: 2, y_lo: 2; y = y_hi * 2 + y_lo), z: 4, core: 2. Of those that a mesh axis runs over, the one named last changes fastest.
Arguments:
- x_in: bfloat16 [2, 6144, 8192], P(None, 'ctx', 'head'), as said below
- z_in: bfloat16 [2, 6144, 8192], P(None, 'ctx', 'head'), may hold values from -6 to 6
- bc_in: bfloat16 [2, 6144, 2, 1024], P(None, 'ctx', None, 'head'), may hold values from -6 to 6
- conv_x: float32 [4, 8192], P(None, 'head'), may hold values from -3 to 3
- conv_bc: float32 [4, 2, 1024], P(None, None, 'head'), may hold values from -3 to 3
- dt_raw: float32 [2, 128, 6144], P(None, 'head', 'ctx'), as said below
- a_log: float32 [128], P('head'), as said below
- skip_scale: float32 [128], P('head'), may hold values from 0.3 to 3
- norm_gain: float32 [8192], P('head'), may hold values from 0.25 to 1.75
- out_weight: bfloat16 [8192, 8192], P('head'), may hold values from -0.09375 to 0.09375
Outputs:
- layer_out: bfloat16 [2, 6144, 8192], P(None, 'ctx', 'head')
Inputs may be any that keep to these rules, and one draw needn't show every extreme that they name: `x_in`: one value a position and channel. `dt_raw`: one value a sequence, head and position. `a_log`: one value a head.
All inputs are finite; a program needn't handle non-finite values.
Results may differ from a plain program's by a relative error of at most 0.034.
Values may be sent and summed in bfloat16 or wider, within the bound.
A program may use at most 128 MiB of HBM per device.

v0:
```python
import jax
import jax.numpy as jnp
from jax import lax
from jax.sharding import PartitionSpec as P

HEAD_DIM = 64
STATE = 128
KW = 4
HALF = 192


def entering(shard, axis, combine, identity, reverse):
    size, mine = (lax.axis_size(axis), lax.axis_index(axis))
    everything = jax.tree.map(
        lambda part, kind: lax.all_gather(part.astype(kind), axis),
        shard,
        jax.tree.map(lambda a: jnp.bfloat16 if a.dtype == jnp.float32 else a.dtype, shard),
    )
    start = jax.tree.map(
        lambda part, zero: jnp.broadcast_to(jnp.asarray(zero, part.dtype), part.shape),
        shard,
        identity,
    )

    def step(k, before):
        at = size - 1 - k if reverse else k
        reached = at > mine if reverse else at < mine
        new = combine(
            before, jax.tree.map(lambda part, own: part[at].astype(own.dtype), everything, shard)
        )
        return jax.tree.map(lambda a, b: jnp.where(reached, a, b), new, before)

    return lax.fori_loop(0, size, step, start)


def shifted(block, axis, distance):
    devices = range(lax.axis_size(axis))
    route = [(i - distance, i) for i in devices if i - distance in devices]
    return lax.ppermute(block, axis, route)


def sigmoid_gate(values):
    return values / (1.0 + jnp.exp(-values))


def compose(earlier, later):
    return (earlier[0] * later[0], later[0][..., None, None] * earlier[1] + later[1])


def chain_entries(block_decay, update):
    lower_pair = (block_decay[:, 0], update[:, 0])
    upper_pair = (block_decay[:, 1], update[:, 1])
    identity_pair = (jnp.ones_like(lower_pair[0]), jnp.zeros_like(lower_pair[1]))
    into_lower = entering(lower_pair, "ctx", compose, identity_pair, False)
    through_lower = compose(into_lower, lower_pair)
    last_flag = lax.axis_index("ctx") == lax.axis_size("ctx") - 1
    joined_pair = compose(through_lower, upper_pair)
    seeded = (
        jnp.where(last_flag, joined_pair[0], upper_pair[0]),
        jnp.where(last_flag, joined_pair[1], upper_pair[1]),
    )
    after_upper = entering(seeded, "ctx", compose, identity_pair, True)
    into_upper = jnp.where(last_flag, through_lower[1], after_upper[1])
    return jnp.stack([into_lower[1], into_upper], axis=1)


def mixer(
    x_part, z_part, bc_part, conv_x, conv_bc, dt_part, a_log, skip_scale, norm_gain, out_weight
):
    seq_count, tok_count, inner_cols = x_part.shape
    group_cols = bc_part.shape[3]
    heads_here = a_log.shape[0]
    groups_here = group_cols // STATE
    per_group = heads_here // groups_here
    block_count = 2 * seq_count
    lag_rows = KW - 1
    joined = jnp.concatenate(
        [x_part, bc_part.reshape(seq_count, tok_count, 2 * group_cols)], axis=2
    )
    halves = joined.reshape(seq_count, 2, HALF, joined.shape[2])
    tail_rows = halves[:, :, HALF - lag_rows :]
    from_lower = shifted(tail_rows[:, 0], "ctx", 1)
    from_upper = shifted(tail_rows[:, 1], "ctx", -1)
    last_flag = lax.axis_index("ctx") == lax.axis_size("ctx") - 1
    upper_lead = jnp.where(last_flag, tail_rows[:, 0], from_upper)
    padded = jnp.concatenate([jnp.stack([from_lower, upper_lead], axis=1), halves], axis=2)
    conv_taps = jnp.concatenate([conv_x, conv_bc.reshape(KW, 2 * group_cols)], axis=1)
    summed = jnp.zeros(halves.shape, jnp.float32)
    for tap_index in range(KW):
        summed = summed + conv_taps[tap_index] * padded[:, :, tap_index : tap_index + HALF].astype(
            jnp.float32
        )
    conv_out = sigmoid_gate(summed).astype(jnp.bfloat16)
    xs_all = conv_out[..., :inner_cols].reshape(block_count, HALF, heads_here, HEAD_DIM)
    bs_all = conv_out[..., inner_cols : inner_cols + group_cols].reshape(
        block_count, HALF, groups_here, STATE
    )
    cs_all = conv_out[..., inner_cols + group_cols :].reshape(block_count, HALF, groups_here, STATE)
    step_size = (
        jax.nn.softplus(dt_part)
        .reshape(seq_count, heads_here, 2, HALF)
        .transpose(0, 2, 1, 3)
        .reshape(block_count, heads_here, HALF)
    )
    cumulative = jnp.cumsum(step_size * (-jnp.exp(a_log))[None, :, None], axis=2)
    causal = jnp.tril(jnp.ones((HALF, HALF), dtype=bool))
    scores = jnp.einsum("bqgn,bugn->bgqu", cs_all, bs_all, preferred_element_type=jnp.float32)
    gap_matrix = cumulative[:, :, :, None] - cumulative[:, :, None, :]
    factor = jnp.where(causal, jnp.exp(jnp.where(causal, gap_matrix, 0.0)), 0.0)
    factor = factor.reshape(block_count, groups_here, per_group, HALF, HALF)
    step_cols = step_size.reshape(block_count, groups_here, per_group, 1, HALF)
    weights = (
        (scores[:, :, None] * factor * step_cols)
        .reshape(block_count, heads_here, HALF, HALF)
        .astype(jnp.bfloat16)
    )
    intra_part = jnp.einsum("bhqu,buhp->bqhp", weights, xs_all, preferred_element_type=jnp.float32)
    tail_decay = jnp.exp(cumulative[:, :, -1:] - cumulative) * step_size
    scaled = (tail_decay.transpose(0, 2, 1)[..., None] * xs_all).astype(jnp.bfloat16)
    update = jnp.einsum(
        "bugkp,bugn->bgkpn",
        scaled.reshape(block_count, HALF, groups_here, per_group, HEAD_DIM),
        bs_all,
        preferred_element_type=jnp.float32,
    )
    update = update.reshape(block_count, heads_here, HEAD_DIM, STATE)
    block_decay = jnp.exp(cumulative[:, :, -1])
    entries = chain_entries(
        block_decay.reshape(seq_count, 2, heads_here),
        update.reshape(seq_count, 2, heads_here, HEAD_DIM, STATE),
    )
    entry_low = entries.reshape(block_count, groups_here, per_group, HEAD_DIM, STATE).astype(
        jnp.bfloat16
    )
    carried = jnp.einsum(
        "bqgn,bgkpn->bqgkp", cs_all, entry_low, preferred_element_type=jnp.float32
    ).reshape(block_count, HALF, heads_here, HEAD_DIM)
    carried = jnp.exp(cumulative).transpose(0, 2, 1)[..., None] * carried
    ssm_out = intra_part + carried + skip_scale[None, None, :, None] * xs_all
    gated_out = ssm_out.reshape(seq_count, tok_count, inner_cols) * sigmoid_gate(
        z_part.astype(jnp.float32)
    )
    grouped = gated_out.reshape(seq_count, tok_count, groups_here, inner_cols // groups_here)
    spread = jnp.mean(grouped * grouped, axis=3, keepdims=True)
    normed = (
        (grouped * lax.rsqrt(spread + 1e-05)).reshape(seq_count * tok_count, inner_cols) * norm_gain
    ).astype(jnp.bfloat16)
    summed_out = lax.psum_scatter(
        lax.dot_general(
            out_weight, normed, (((0,), (1,)), ((), ())), preferred_element_type=jnp.float32
        ).astype(jnp.bfloat16),
        "head",
        scatter_dimension=0,
        tiled=True,
    ).astype(jnp.float32)
    return summed_out.T.reshape(seq_count, tok_count, summed_out.shape[0]).astype(jnp.bfloat16)


def body(x_in, z_in, bc_in, conv_x, conv_bc, dt_raw, a_log, skip_scale, norm_gain, out_weight):
    return mixer(
        x_in, z_in, bc_in, conv_x, conv_bc, dt_raw, a_log, skip_scale, norm_gain, out_weight
    )


def solution(mesh):
    in_specs = (
        P(None, "ctx", "head"),
        P(None, "ctx", "head"),
        P(None, "ctx", None, "head"),
        P(None, "head"),
        P(None, None, "head"),
        P(None, "head", "ctx"),
        P("head"),
        P("head"),
        P("head"),
        P("head", None),
    )
    out_specs = P(None, "ctx", "head")
    return jax.shard_map(body, mesh=mesh, in_specs=in_specs, out_specs=out_specs, check_vma=False)
```

profile of v0, /device:TPU:1, one launch (start us, length us, event | category | flops | bytes accessed | tf_op | source)
XLA Modules:
  0.0 391.8 jit_solution(13414120632968366925)
XLA Ops:
  6.5 1.4 concatenate.19
  8.7 3.3 collective-permute-start.1
  14.4 2.3 reduce-window.6
  18.0 3.2 collective-permute-start
  22.6 2.4 divide_convert_fusion
  25.3 2.5 copy.60
  27.8 2.3 fusion.16
  31.2 21.9 %all-gather = bf16[32,1,16]{2,1,0:T(2,128)(2,1)S(1)} all-gather(bf16[2,1,16]{2,1,0:T(2,128)(2,1)S(1)} %slice.160), channel_id=2, replica_groups=mesh['ctx'=16,'head'=8] {'ctx'}, dimensions={0}, use_global_device_ids=true | all-gather | bytes 1088 | tf_op jit(solution)/shard_map/all_gather | solution.py:15
  53.7 34.4 %all-gather.8.cloned.1.call-done = bf16[32,1,16,64,128]{4,3,2,1,0:T(8,128)(2,1)} async-done(((bf16[2,1,16,64,128]{4,3,2,1,0:T(8,128)(2,1)}), bf16[32,1,16,64,128]{4,3,2,1,0:T(8,128)(2,1)}) %all-gather.8.cloned.1.call-update) | async-done | bytes 8388624 | tf_op jit(solution)/shard_map/all_gather | solution.py:15
  88.1 21.7 %while.32 = (s32[]{:T(128)}, f32[2,16]{1,0:T(2,128)S(1)}, f32[2,16,64,128]{3,2,1,0:T(8,128)S(1)}, s32[]{:T(128)}, bf16[16,2,16]{2,1,0:T(2,128)(2,1)S(1)}, /*inde...) while((s32[]{:T(128)}, f32[2,16]{1,0:T(2,128)S(1)}, f32[2,16,64,128]{3,2,1,0:T(8,128)S(1)}, ...), condition=%wide.region_3.4_spmd.clone, body=%wide.region_2.3_spmd.clone.sunk | while | flops 1310884 | bytes 2622199 | solution.py:33
  109.9 2.1 convert_bitcast_fusion
  112.0 4.9 %copy.68 = bf16[2,384,1024]{1,0,2:T(2,128)(2,1)} copy(bf16[2,384,1024]{2,1,0:T(8,128)(2,1)} %param.15) | data formatting | bytes 3145728 | tf_op args[1]
  117.3 19.1 %all-gather.4 = bf16[16,2,16]{2,1,0:T(2,128)(2,1)S(1)} all-gather(bf16[1,2,16]{2,1,0:T(2,128)(2,1)S(1)} %fusion.29), channel_id=4, replica_groups=mesh['ctx'=16,'head'=8] {'ctx'}, dimensions={0}, use_global_device_ids=true | all-gather | bytes 1088 | tf_op jit(solution)/shard_map/all_gather | solution.py:15
  136.5 28.8 %all-gather.10.cloned.1.call-done = bf16[32,16,64,128]{3,2,1,0:T(8,128)(2,1)} async-done(((bf16[2,16,64,128]{3,2,1,0:T(8,128)(2,1)}), bf16[32,16,64,128]{3,2,1,0:T(8,128)(2,1)}) %all-gather.10.cloned.1.call-update) | async-done | bytes 8388624 | tf_op jit(solution)/shard_map/all_gather | solution.py:15
  165.3 21.6 %while.33 = (s32[]{:T(128)}, f32[2,16,64,128]{3,2,1,0:T(8,128)S(1)}, s32[]{:T(128)}, bf16[16,2,16]{2,1,0:T(2,128)(2,1)S(1)}, bf16[16,2,16,64,128]{4,3,2,1,0:T(8,...) while((s32[]{:T(128)}, f32[2,16,64,128]{3,2,1,0:T(8,128)S(1)}, s32[]{:T(128)}, ...), condition=%wide.region_5.6_spmd.clone, body=%wide.region_4.5_spmd.clone.sunk | while | flops 1310760 | bytes 2621927 | solution.py:33
  166.6 1.3 fusion.48
  168.0 1.3 fusion.48
  186.8 1.5 fusion.21
  190.1 4.6 %fusion.11 = f32[4,192,16,64]{1,3,2,0:T(8,128)S(1)} fusion(bf16[4,192,16,64]{1,3,2,0:T(8,128)(2,1)S(1)} %bitcast.140, f32[4,16,64,192]{3,2,1,0:T(8,128)S(1)} %fusion.37, f32[4,16,192]{2,1,0:T(8,128)S(1)} %bitcast.151, f32[4,16,192]{2,1,0:T(8,128)S(1)} %copy-done.7, f32[4,192,192]{2,1,0:T(8,128)S(1)} %fusion.36, pred[192,192]{1,0:T(8,128)(4,1)S(1)} %iota_compare_fusion, ...), kind=kOutput, calls=%fused_computation.20 | convolution fusion | flops 320077824 | bytes 8638528 | tf_op jit(solution)/shard_map/bhqu,buhp->bqhp/dot_general | solution.py:117
  194.6 4.7 %copy.67 = f32[4,192,16,64]{1,0,3,2:T(4,128)} copy(f32[4,192,16,64]{1,3,2,0:T(8,128)S(1)} %fusion.11) | data formatting | bytes 6291456 | tf_op jit(solution)/shard_map/add | solution.py:139
  199.4 5.5 %reshape.164 = f32[2,384,1024]{1,0,2:T(2,128)S(1)} reshape(f32[4,192,16,64]{1,0,3,2:T(4,128)} %copy.67) | data formatting | bytes 6291456 | tf_op jit(solution)/shard_map/reshape | solution.py:140
  204.8 5.6 %multiply_reduce_fusion = (f32[2,384]{1,0:T(2,128)S(1)}, f32[2,384,1024]{1,0,2:T(2,128)S(1)}) fusion(f32[2,384,1024]{1,0,2:T(2,128)S(1)} %reshape.164, bf16[2,384,1024]{1,0,2:T(2,128)(2,1)} %copy.68), kind=kLoop, calls=%fused_computation.30 | loop fusion | flops 5504256 | bytes 7867392 | tf_op jit(solution)/shard_map/reduce_sum | solution.py:144
  211.4 21.8 %fusion.2 = bf16[8192,768]{0,1:T(8,128)(2,1)} fusion(bf16[1024,8192]{1,0:T(8,128)(2,1)} %param.23, f32[768,1024]{0,1:T(8,128)S(1)} %bitcast.142, f32[1024]{0:T(1024)S(1)} %copy-done.11), kind=kOutput, calls=%fused_computation.9 | convolution fusion | flops 12892766208 | bytes 32509952 | tf_op jit(solution)/shard_map/dot_general | solution.py:149
  233.2 152.0 %reduce-scatter.2.cloned.1.call-done = bf16[1024,768]{0,1:T(8,128)(2,1)} async-done(((bf16[8192,768]{0,1:T(8,128)(2,1)}), bf16[1024,768]{0,1:T(8,128)(2,1)}) %reduce-scatter.2.cloned.1.call-update) | async-done | bytes 1572880 | tf_op jit(solution)/shard_map/reduce_scatter | solution.py:148
  (151 shorter events, 50.2 us)
Async XLA Ops:
  6.5 11.4 %copy-start = (bf16[2,384,1024]{2,1,0:T(8,128)(2,1)S(1)}, bf16[2,384,1024]{2,1,0:T(8,128)(2,1)}, u32[]{:S(2)}) copy-start(bf16[2,384,1024]{2,1,0:T(8,128)(2,1)} %param.14) | copy-start | bytes 4718596
  6.5 11.4 %copy-start.10 = (f32[4,2,128]{2,1,0:T(2,128)S(1)}, f32[4,2,128]{2,1,0:T(2,128)}, u32[]{:S(2)}) copy-start(f32[4,2,128]{2,1,0:T(2,128)} %param.18) | copy-start | bytes 12292
  6.5 81.6 %all-gather.8.cloned.1.call-start = ((), (), s32[]{:S(2)}) async-start(), calls=%async_computation.2 | async-start | bytes 8912896 | tf_op jit(solution)/shard_map/all_gather | solution.py:15
  8.7 9.3 %collective-permute-start.1 = (bf16[2,3,1280]{2,1,0:T(4,128)(2,1)S(1)}, bf16[2,3,1280]{2,1,0:T(4,128)(2,1)S(1)}, u32[]{:S(2)}, u32[]{:S(2)}) collective-permute-start(bf16[2,3,1280]{2,1,0:T(4,128)(2,1)S(1)} %fusion.24), channel_id=1, source_target_pairs={{8,0},{16,8},{24,16},{32,24},{40,32},{48,40},{56,48},{64,56},{72,6... | collective-permute-start | bytes 46088 | tf_op jit(solution)/shard_map/ppermute | solution.py:39
  14.3 10.7 %copy-start.4 = (f32[2,32,192]{2,1,0:T(8,128)}, f32[2,32,192]{2,1,0:T(8,128)S(1)}, u32[]{:S(2)}) copy-start(f32[2,32,192]{2,1,0:T(8,128)S(1)} %pad_maximum_fusion.2) | copy-start | bytes 147460
  18.0 4.1 %collective-permute-start = (bf16[2,3,1280]{2,1,0:T(4,128)(2,1)S(1)}, bf16[2,3,1280]{2,1,0:T(4,128)(2,1)S(1)}, u32[]{:S(2)}, u32[]{:S(2)}) collective-permute-start(bf16[2,3,1280]{2,1,0:T(4,128)(2,1)S(1)} %get-tuple-element.320), channel_id=1, source_target_pairs={{0,8},{8,16},{16,24},{24,32},{32,40},{40,48},{48,56},{56,64},{64,7... | collective-permute-start | bytes 46088 | tf_op jit(solution)/shard_map/ppermute | solution.py:39
  30.1 79.7 %copy-start.1 = (f32[4,16,64,128]{3,2,1,0:T(8,128)}, f32[4,16,64,128]{3,2,1,0:T(8,128)S(1)}, u32[]{:S(2)}) copy-start(f32[4,16,64,128]{3,2,1,0:T(8,128)S(1)} %fusion.16) | copy-start | bytes 6291460
  31.1 134.1 %all-gather.10.cloned.1.call-start = ((), (), s32[]{:S(2)}) async-start(), calls=%async_computation.3 | async-start | bytes 8912896 | tf_op jit(solution)/shard_map/all_gather | solution.py:15
  109.9 7.4 %copy-start.8 = (f32[2,1,16]{2,1,0:T(1,128)S(1)}, f32[2,1,16]{2,1,0:T(1,128)}, u32[]{:S(2)}) copy-start(f32[2,1,16]{2,1,0:T(1,128)} %get-tuple-element.330) | copy-start | bytes 388
  109.9 7.4 %copy-start.9 = (f32[2,1,16]{2,1,0:T(1,128)S(1)}, f32[2,1,16]{2,1,0:T(1,128)}, u32[]{:S(2)}) copy-start(f32[2,1,16]{2,1,0:T(1,128)} %get-tuple-element.331) | copy-start | bytes 388
  112.0 273.3 %reduce-scatter.2.cloned.1.call-start = ((), (), s32[]{:S(2)}) async-start(), calls=%async_computation.1 | async-start | bytes 14155776 | tf_op jit(solution)/shard_map/reduce_scatter | solution.py:148
  186.8 1.5 copy-start.3
  188.5 1.6 copy-start.2
  188.5 1.6 copy-start.5
  188.5 1.6 copy-start.6
  188.5 1.6 copy-start.7
  188.5 1.6 copy-start.12
  210.7 0.7 copy-start.11
Sparse Core Ops, SparseCore 0:
  31.2 56.8 all-gather.7
  112.1 53.1 all-gather.9
  233.3 151.8 reduce-scatter.1
where the time goes:
time: 394 us; the launch traced here: 392 us
  waiting for transfers between devices  216 us (55%)
  other arithmetic  60.1 us (15%)
  blocking collectives  41.1 us (10%)
  matrix products  29.6 us (8%)
  local copies, waits for them, and re-layouts  23.6 us (6%)
  between operations  13.5 us (3%)
  starting transfers between devices  6.6 us (2%)
    reduce_scatter x1, waiting for transfers between devices, mixer(): lax.psum_scatter(lax.dot_general(out_weight, normed, (((0,), (1,)), ((),...  152 us
    all_gather x2, waiting for transfers between devices, entering(): lax.all_gather(part.astype(kind), axis)  63.2 us
    select_n x48, other arithmetic, step(): return jax.tree.map(lambda a, b: jnp.where(reached, a, b), new, before)  41.9 us
    all_gather x2, blocking collectives, entering(): lax.all_gather(part.astype(kind), axis)  41.1 us
    dot_general x1, matrix products, mixer(): lax.dot_general(out_weight, normed, (((0,), (1,)), ((), ())), preferred_e...  21.8 us
  transfers between devices with their start and end apart: 5, of which 4 were waited for; matrix products, arithmetic and copies ran while one was open for 3% of the time, Pallas kernels for 0%

commit v1 on v0

--- a/solution.py
+++ b/solution.py
@@ -7,30 +7,6 @@
 STATE = 128
 KW = 4
 HALF = 192
-
-
-def entering(shard, axis, combine, identity, reverse):
-    size, mine = (lax.axis_size(axis), lax.axis_index(axis))
-    everything = jax.tree.map(
-        lambda part, kind: lax.all_gather(part.astype(kind), axis),
-        shard,
-        jax.tree.map(lambda a: jnp.bfloat16 if a.dtype == jnp.float32 else a.dtype, shard),
-    )
-    start = jax.tree.map(
-        lambda part, zero: jnp.broadcast_to(jnp.asarray(zero, part.dtype), part.shape),
-        shard,
-        identity,
-    )
-
-    def step(k, before):
-        at = size - 1 - k if reverse else k
-        reached = at > mine if reverse else at < mine
-        new = combine(
-            before, jax.tree.map(lambda part, own: part[at].astype(own.dtype), everything, shard)
-        )
-        return jax.tree.map(lambda a, b: jnp.where(reached, a, b), new, before)
-
-    return lax.fori_loop(0, size, step, start)
 
 
 def shifted(block, axis, distance):
@@ -43,25 +19,28 @@
     return values / (1.0 + jnp.exp(-values))
 
 
-def compose(earlier, later):
-    return (earlier[0] * later[0], later[0][..., None, None] * earlier[1] + later[1])
+def chain_entries(block_decay, update):
+    size = lax.axis_size("ctx")
+    seq_count, _, heads_here, rows, cols = update.shape
+    owned = heads_here // size
 
+    def spread(values):
+        split = values.reshape((seq_count, 2, size, owned) + values.shape[3:])
+        return lax.all_to_all(jnp.moveaxis(split, 2, 0), "ctx", 0, 0)
 
-def chain_entries(block_decay, update):
-    lower_pair = (block_decay[:, 0], update[:, 0])
-    upper_pair = (block_decay[:, 1], update[:, 1])
-    identity_pair = (jnp.ones_like(lower_pair[0]), jnp.zeros_like(lower_pair[1]))
-    into_lower = entering(lower_pair, "ctx", compose, identity_pair, False)
-    through_lower = compose(into_lower, lower_pair)
-    last_flag = lax.axis_index("ctx") == lax.axis_size("ctx") - 1
-    joined_pair = compose(through_lower, upper_pair)
-    seeded = (
-        jnp.where(last_flag, joined_pair[0], upper_pair[0]),
-        jnp.where(last_flag, joined_pair[1], upper_pair[1]),
-    )
-    after_upper = entering(seeded, "ctx", compose, identity_pair, True)
-    into_upper = jnp.where(last_flag, through_lower[1], after_upper[1])
-    return jnp.stack([into_lower[1], into_upper], axis=1)
+    decays = spread(block_decay)
+    updates = spread(update.astype(jnp.bfloat16))
+    order = [(c, 0) for c in range(size)] + [(c, 1) for c in reversed(range(size))]
+    state = jnp.zeros((seq_count, owned, rows, cols), jnp.float32)
+    entry = [[None, None] for _ in range(size)]
+    for c, half in order:
+        entry[c][half] = state.astype(jnp.bfloat16)
+        state = decays[c, :, half][..., None, None] * state + updates[c, :, half].astype(
+            jnp.float32
+        )
+    stacked = jnp.stack([jnp.stack(pair, axis=1) for pair in entry])
+    back = lax.all_to_all(stacked, "ctx", 0, 0)
+    return jnp.moveaxis(back, 0, 2).reshape(seq_count, 2, heads_here, rows, cols)
 
 
 def mixer(

time: 394 us -> 300 us (0.76)
  blocking collectives: 41.1 us -> 0 us
  waiting for transfers between devices: 216 us -> 179 us
  other arithmetic: 60.1 us -> 29.8 us
  starting transfers between devices: 6.6 us -> 23.5 us
    all_gather x2 -> x0, waiting for transfers between devices: 63.2 us -> none  [entering(): lax.all_gather(part.astype(kind), axis)]
    select_n x48 -> x0, other arithmetic: 41.9 us -> none  [step(): return jax.tree.map(lambda a, b: jnp.where(reached, a, b), new, before)]
    all_gather x2 -> x0, blocking collectives: 41.1 us -> none  [entering(): lax.all_gather(part.astype(kind), axis)]
    all_to_all x0 -> x3, waiting for transfers between devices: none -> 24.8 us  [the longest x2 13.8 us: spread(): return lax.all_to_all(jnp.moveaxis(split, 2, 0), 'ctx', 0, 0)]
    all_to_all x0 -> x3, starting transfers between devices: none -> 19.4 us  [the longest x2 15.1 us: spread(): return lax.all_to_all(jnp.moveaxis(split, 2, 0), 'ctx', 0, 0)]
    unnamed x4 -> x14, other arithmetic: 0.01 us -> 8.71 us
    convert_element_type x32 -> x16, other arithmetic: 0.25 us -> 5.12 us  [chain_entries(): entry[c][half] = state.astype(jnp.bfloat16)]
  transfers between devices with their start and end apart: 5 -> 6, of which waited for: 4 -> 5; matrix products, arithmetic and copies ran while one was open for 3% -> 6% of each run, Pallas kernels for 0% -> 0%
where the time goes in v1:
time: 300 us; the launch traced here: 299 us
  waiting for transfers between devices  179 us (60%)
  matrix products  30.5 us (10%)
  other arithmetic  29.8 us (10%)
  starting transfers between devices  23.5 us (8%)
  local copies, waits for them, and re-layouts  22.1 us (7%)
  between operations  13.8 us (5%)
    reduce_scatter x1, waiting for transfers between devices, mixer(): lax.psum_scatter(lax.dot_general(out_weight, normed, (((0,), (1,)), ((),...  150 us
    dot_general x1, matrix products, mixer(): lax.dot_general(out_weight, normed, (((0,), (1,)), ((), ())), preferred_e...  21.8 us
    all_to_all x2, starting transfers between devices, spread(): return lax.all_to_all(jnp.moveaxis(split, 2, 0), 'ctx', 0, 0)  15.1 us
    all_to_all x2, waiting for transfers between devices, spread(): return lax.all_to_all(jnp.moveaxis(split, 2, 0), 'ctx', 0, 0)  13.8 us
    all_to_all x1, waiting for transfers between devices, chain_entries(): back = lax.all_to_all(stacked, 'ctx', 0, 0)  11 us
    unnamed x14, other arithmetic  8.71 us
  transfers between devices with their start and end apart: 6, of which 5 were waited for; matrix products, arithmetic and copies ran while one was open for 6% of the time, Pallas kernels for 0%

profile of v1, /device:TPU:1, one launch (start us, length us, event | category | flops | bytes accessed | tf_op | source)
XLA Modules:
  0.0 298.9 jit_solution(2160184824172741152)
XLA Ops:
  8.3 2.3 reduce-window.6
  11.8 7.8 %all-to-all-start = ((f32[16,2,2,1]{2,1,3,0:T(2,128)}), f32[16,2,2,1]{2,1,3,0:T(2,128)S(1)}, u32[]{:S(2)}, u32[]{:S(2)}) async-start(f32[16,2,2,1]{2,1,3,0:T(2,128)} %copy.152), calls=%async_computation | async-start | bytes 32768 | tf_op jit(solution)/shard_map/all_to_all | solution.py:29
  19.7 1.2 concatenate.19
  21.7 2.0 collective-permute-start.1
  23.8 2.9 collective-permute-done.1
  26.8 1.9 collective-permute-start
  28.8 1.1 collective-permute-done
  30.4 2.4 divide_convert_fusion
  33.1 2.5 copy.147
  35.7 2.3 fusion.18
  38.0 1.0 copy.230
  39.0 7.2 %all-to-all-start.1 = ((bf16[16,2,2,1,64,128]{5,4,2,1,3,0:T(8,128)(2,1)}), bf16[16,2,2,1,64,128]{5,4,2,1,3,0:T(8,128)(2,1)S(1)}, u32[]{:S(2)}, u32[]{:S(2)}) async-start(bf16[16,2,2,1,64,128]{5,4,2,1,3,0:T(8,128)(2,1)} %bitcast.427), calls=%async_computation.1 | async-start | bytes 2097152 | tf_op jit(solution)/shard_map/all_to_all | solution.py:29
  47.2 1.0 slice_reduce_fusion.34
  48.2 13.8 %all-to-all-done.1 = bf16[16,2,2,1,64,128]{5,4,2,1,3,0:T(8,128)(2,1)S(1)} async-done(((bf16[16,2,2,1,64,128]{5,4,2,1,3,0:T(8,128)(2,1)}), bf16[16,2,2,1,64,128]{5,4,2,1,3,0:T(8,128)(2,1)S(1)}, u32[]{:S(2)}, u32[]{:S(2)}) %all-to-all-start.1) | async-done | bytes 1048608 | tf_op jit(solution)/shard_map/all_to_all | solution.py:29
  77.3 4.3 %all-to-all-start.2 = ((bf16[16,2,2,1,64,128]{5,4,1,2,3,0:T(8,128)(2,1)}), bf16[16,2,2,1,64,128]{5,4,1,2,3,0:T(8,128)(2,1)S(1)}, u32[]{:S(2)}, u32[]{:S(2)}) async-start(bf16[16,2,2,1,64,128]{5,4,1,2,3,0:T(8,128)(2,1)} %fusion.35), calls=%async_computation.2 | async-start | bytes 2097152 | tf_op jit(solution)/shard_map/all_to_all | solution.py:42
  81.9 2.9 copy.187
  85.4 1.2 fusion.74
  86.6 11.0 %all-to-all-done.2 = bf16[16,2,2,1,64,128]{5,4,1,2,3,0:T(8,128)(2,1)S(1)} async-done(((bf16[16,2,2,1,64,128]{5,4,1,2,3,0:T(8,128)(2,1)}), bf16[16,2,2,1,64,128]{5,4,1,2,3,0:T(8,128)(2,1)S(1)}, u32[]{:S(2)}, u32[]{:S(2)}) %all-to-all-start.2) | async-done | bytes 1048608 | tf_op jit(solution)/shard_map/all_to_all | solution.py:42
  98.7 4.5 %fusion.9 = f32[4,192,16,64]{1,3,2,0:T(8,128)S(1)} fusion(bf16[4,192,16,64]{1,3,2,0:T(8,128)(2,1)S(1)} %bitcast.441, f32[4,16,64,192]{3,2,1,0:T(8,128)S(1)} %fusion.75, f32[4,16,192]{2,1,0:T(8,128)S(1)} %bitcast.449, f32[4,16,192]{2,1,0:T(8,128)S(1)} %get-tuple-element.92, f32[4,192,192]{2,1,0:T(8,128)S(1)} %copy-done.3, ...), kind=kOutput, calls=%fused_computation.13 | convolution fusion | flops 320077824 | bytes 8638528 | tf_op jit(solution)/shard_map/bhqu,buhp->bqhp/dot_general | solution.py:96
  103.2 4.7 %copy.186 = f32[4,192,16,64]{1,0,3,2:T(4,128)} copy(f32[4,192,16,64]{1,3,2,0:T(8,128)S(1)} %fusion.9) | data formatting | bytes 6291456 | tf_op jit(solution)/shard_map/add | solution.py:118
  108.0 5.5 %reshape.3389 = f32[2,384,1024]{1,0,2:T(2,128)S(1)} reshape(f32[4,192,16,64]{1,0,3,2:T(4,128)} %copy.186) | data formatting | bytes 6291456 | tf_op jit(solution)/shard_map/reshape | solution.py:119
  113.4 5.6 %multiply_reduce_fusion = (f32[2,384]{1,0:T(2,128)S(1)}, f32[2,384,1024]{1,0,2:T(2,128)S(1)}) fusion(f32[2,384,1024]{1,0,2:T(2,128)S(1)} %reshape.3389, bf16[2,384,1024]{1,0,2:T(2,128)(2,1)} %copy.187), kind=kLoop, calls=%fused_computation.23 | loop fusion | flops 5504256 | bytes 7867392 | tf_op jit(solution)/shard_map/reduce_sum | solution.py:123
  120.0 21.8 %fusion = bf16[8192,768]{0,1:T(8,128)(2,1)} fusion(bf16[1024,8192]{1,0:T(8,128)(2,1)} %param.19, f32[768,1024]{0,1:T(8,128)S(1)} %bitcast.439, f32[1024]{0:T(1024)S(1)} %copy-done.15), kind=kOutput, calls=%fused_computation.2 | convolution fusion | flops 12892766208 | bytes 32509952 | tf_op jit(solution)/shard_map/dot_general | solution.py:128
  141.8 150.2 %reduce-scatter.2.cloned.1.call-done = bf16[1024,768]{0,1:T(8,128)(2,1)} async-done(((bf16[8192,768]{0,1:T(8,128)(2,1)}), bf16[1024,768]{0,1:T(8,128)(2,1)}) %reduce-scatter.2.cloned.1.call-update) | async-done | bytes 1572880 | tf_op jit(solution)/shard_map/reduce_scatter | solution.py:127
  (100 shorter events, 23.6 us)
Async XLA Ops:
  6.5 20.2 %copy-start = (bf16[2,384,1024]{2,1,0:T(8,128)(2,1)S(1)}, bf16[2,384,1024]{2,1,0:T(8,128)(2,1)}, u32[]{:S(2)}) copy-start(bf16[2,384,1024]{2,1,0:T(8,128)(2,1)} %param.10) | copy-start | bytes 4718596
  6.5 17.2 %copy-start.5 = (f32[4,1024]{1,0:T(4,128)S(1)}, f32[4,1024]{1,0:T(4,128)}, u32[]{:S(2)}) copy-start(f32[4,1024]{1,0:T(4,128)} %param.13) | copy-start | bytes 49156
  6.5 17.3 %copy-start.11 = (f32[4,2,128]{2,1,0:T(2,128)S(1)}, f32[4,2,128]{2,1,0:T(2,128)}, u32[]{:S(2)}) copy-start(f32[4,2,128]{2,1,0:T(2,128)} %param.14) | copy-start | bytes 12292
  11.8 27.2 %all-to-all-start = ((f32[16,2,2,1]{2,1,3,0:T(2,128)}), f32[16,2,2,1]{2,1,3,0:T(2,128)S(1)}, u32[]{:S(2)}, u32[]{:S(2)}) async-start(f32[16,2,2,1]{2,1,3,0:T(2,128)} %copy.152), calls=%async_computation | async-start | bytes 32768 | tf_op jit(solution)/shard_map/all_to_all | solution.py:29
  21.7 5.1 %collective-permute-start.1 = (bf16[2,3,1280]{2,1,0:T(4,128)(2,1)S(1)}, bf16[2,3,1280]{2,1,0:T(4,128)(2,1)S(1)}, u32[]{:S(2)}, u32[]{:S(2)}) collective-permute-start(bf16[2,3,1280]{2,1,0:T(4,128)(2,1)S(1)} %fusion.56), channel_id=1, source_target_pairs={{8,0},{16,8},{24,16},{32,24},{40,32},{48,40},{56,48},{64,56},{72,6... | collective-permute-start | bytes 46088 | tf_op jit(solution)/shard_map/ppermute | solution.py:15
  26.8 3.1 %collective-permute-start = (bf16[2,3,1280]{2,1,0:T(4,128)(2,1)S(1)}, bf16[2,3,1280]{2,1,0:T(4,128)(2,1)S(1)}, u32[]{:S(2)}, u32[]{:S(2)}) collective-permute-start(bf16[2,3,1280]{2,1,0:T(4,128)(2,1)S(1)} %get-tuple-element.67), channel_id=1, source_target_pairs={{0,8},{8,16},{16,24},{24,32},{32,40},{40,48},{48,56},{56,64},{64,7... | collective-permute-start | bytes 46088 | tf_op jit(solution)/shard_map/ppermute | solution.py:15
  39.0 23.1 %all-to-all-start.1 = ((bf16[16,2,2,1,64,128]{5,4,2,1,3,0:T(8,128)(2,1)}), bf16[16,2,2,1,64,128]{5,4,2,1,3,0:T(8,128)(2,1)S(1)}, u32[]{:S(2)}, u32[]{:S(2)}) async-start(bf16[16,2,2,1,64,128]{5,4,2,1,3,0:T(8,128)(2,1)} %bitcast.427), calls=%async_computation.1 | async-start | bytes 2097152 | tf_op jit(solution)/shard_map/all_to_all | solution.py:29
  48.2 14.0 %copy-start.6 = (f32[2]{0:T(128)}, f32[2]{0:T(128)S(1)}, u32[]{:S(2)}) copy-start(f32[2]{0:T(128)S(1)} %get-tuple-element.12) | copy-start | bytes 28
  48.2 14.0 %copy-start.7 = (f32[2]{0:T(128)}, f32[2]{0:T(128)S(1)}, u32[]{:S(2)}) copy-start(f32[2]{0:T(128)S(1)} %get-tuple-element.13) | copy-start | bytes 28
  48.2 14.1 %copy-start.8 = (f32[2]{0:T(128)}, f32[2]{0:T(128)S(1)}, u32[]{:S(2)}) copy-start(f32[2]{0:T(128)S(1)} %get-tuple-element.15) | copy-start | bytes 28
  48.2 14.1 %copy-start.9 = (f32[2]{0:T(128)}, f32[2]{0:T(128)S(1)}, u32[]{:S(2)}) copy-start(f32[2]{0:T(128)S(1)} %get-tuple-element.17) | copy-start | bytes 28
  62.1 5.0 %copy-start.13 = (f32[2]{0:T(128)S(1)}, f32[2]{0:T(128)}, u32[]{:S(2)}) copy-start(f32[2]{0:T(128)} %get-tuple-element.40) | copy-start | bytes 28
  62.1 5.0 %copy-start.14 = (f32[2]{0:T(128)S(1)}, f32[2]{0:T(128)}, u32[]{:S(2)}) copy-start(f32[2]{0:T(128)} %get-tuple-element.41) | copy-start | bytes 28
  62.1 5.1 %copy-start.10 = (f32[2]{0:T(128)S(1)}, f32[2]{0:T(128)}, u32[]{:S(2)}) copy-start(f32[2]{0:T(128)} %get-tuple-element.30) | copy-start | bytes 28
  62.1 5.1 %copy-start.12 = (f32[2]{0:T(128)S(1)}, f32[2]{0:T(128)}, u32[]{:S(2)}) copy-start(f32[2]{0:T(128)} %get-tuple-element.11) | copy-start | bytes 28
  62.3 19.6 %copy-start.2 = (bf16[2,384,1024]{2,1,0:T(8,128)(2,1)S(1)}, bf16[2,384,1024]{2,1,0:T(8,128)(2,1)}, u32[]{:S(2)}) copy-start(bf16[2,384,1024]{2,1,0:T(8,128)(2,1)} %param.11) | copy-start | bytes 4718596
  77.3 20.2 %all-to-all-start.2 = ((bf16[16,2,2,1,64,128]{5,4,1,2,3,0:T(8,128)(2,1)}), bf16[16,2,2,1,64,128]{5,4,1,2,3,0:T(8,128)(2,1)S(1)}, u32[]{:S(2)}, u32[]{:S(2)}) async-start(bf16[16,2,2,1,64,128]{5,4,1,2,3,0:T(8,128)(2,1)} %fusion.35), calls=%async_computation.2 | async-start | bytes 2097152 | tf_op jit(solution)/shard_map/all_to_all | solution.py:42
  81.6 210.4 %reduce-scatter.2.cloned.1.call-start = ((), (), s32[]{:S(2)}) async-start(), calls=%async_computation.4 | async-start | bytes 14155776 | tf_op jit(solution)/shard_map/reduce_scatter | solution.py:127
  86.6 11.8 %copy-start.1 = (bf16[2,2,192,1024]{2,3,1,0:T(8,128)(2,1)S(1)}, bf16[2,2,192,1024]{2,3,1,0:T(8,128)(2,1)}, u32[]{:S(2)}) copy-start(bf16[2,2,192,1024]{2,3,1,0:T(8,128)(2,1)} %copy.147) | copy-start | bytes 4718596
  86.6 11.8 %copy-start.16 = (f32[16]{0:T(128)S(1)}, f32[16]{0:T(128)}, u32[]{:S(2)}) copy-start(f32[16]{0:T(128)} %param.17) | copy-start | bytes 196
  97.6 1.1 copy-start.3
  97.6 1.1 copy-start.4
  119.3 0.7 copy-start.15
Sparse Core Ops, SparseCore 0:
  142.0 150.0 reduce-scatter.1

commit v2 on v1

--- a/solution.py
+++ b/solution.py
@@ -1,12 +1,280 @@
 import jax
 import jax.numpy as jnp
 from jax import lax
+from jax.experimental import pallas as pl
+from jax.experimental.pallas import tpu as pltpu
 from jax.sharding import PartitionSpec as P
 
 HEAD_DIM = 64
 STATE = 128
 KW = 4
 HALF = 192
+MESH = pl.DeviceIdType.MESH
+REACH = (2, 1, 3, 0)
+
+
+def place():
+    c, h = lax.axis_index("ctx"), lax.axis_index("head")
+    return c // 4, (c // 2) % 2, c % 2, h // 2, h % 2
+
+
+def device(z, y_lo, core, x, y_hi):
+    return (z * 4 + y_lo * 2 + core, x * 2 + y_hi)
+
+
+def greet(devices):
+    barrier = pltpu.get_barrier_semaphore()
+    for one in devices:
+        pl.semaphore_signal(barrier, inc=1, device_id=one, device_id_type=MESH)
+    pl.semaphore_wait(barrier, len(devices))
+
+
+def remote(src, dst, send_sem, recv_sem, target):
+    return pltpu.make_async_remote_copy(
+        src_ref=src,
+        dst_ref=dst,
+        send_sem=send_sem,
+        recv_sem=recv_sem,
+        device_id=target,
+        device_id_type=MESH,
+    )
+
+
+def weight_kernel(w_ref, wr_ref, in_s, in_r, z_s, z_r, far_s, far_r, core_s, core_r):
+    z, y_lo, core, x, y_hi = place()
+    partner = device(z, 1 - y_lo, core, x, 1 - y_hi)
+    up = device((z + 1) % 4, y_lo, core, x, y_hi)
+    down = device((z + 3) % 4, y_lo, core, x, y_hi)
+    other = device(z, y_lo, 1 - core, x, y_hi)
+    depth, cols = wr_ref.shape[1:]
+    part = depth // 8
+
+    def rows(step, which):
+        return pl.ds(pl.multiple_of((((z + step) % 4) * 2 + which) * part, part), part)
+
+    greet([partner, up, down, other])
+    mine = rows(0, core)
+    started = []
+
+    def start(copy):
+        copy.start()
+        started.append(copy)
+        return copy
+
+    def pair(g, step, send_sem, recv_sem, target):
+        here = wr_ref.at[pl.ds(2 * g, 2), rows(step, core)]
+        return remote(here, here, send_sem, recv_sem, target)
+
+    ins = []
+    for d in range(4):
+        block = 2 * ((x + REACH[d]) % 4) + 1 - y_hi
+        src = w_ref.at[mine, pl.ds(pl.multiple_of(block * cols, cols), cols)]
+        ins.append(start(remote(src, wr_ref.at[d, mine], in_s.at[d], in_r.at[d], partner)))
+    near, across = {}, []
+    for g in range(2):
+        ins[2 * g].wait_recv()
+        ins[2 * g + 1].wait_recv()
+        near[g, 0] = start(pair(g, 0, z_s.at[g, 0], z_r.at[g, 0], up))
+        near[g, 1] = start(pair(g, 0, z_s.at[g, 1], z_r.at[g, 1], down))
+        across.append(start(pair(g, 0, core_s.at[g, 0], core_r.at[g, 0], other)))
+    far = {}
+    for g in range(2):
+        for way in range(2):
+            near[g, way].wait_recv()
+            step = 3 if way == 0 else 1
+            half = wr_ref.at[2 * g + way, rows(step, core)]
+            far[g, way] = start(
+                remote(
+                    half, half, far_s.at[g, way], far_r.at[g, way], up if way == 0 else down
+                )
+            )
+            across.append(
+                start(pair(g, step, core_s.at[g, 1 + way], core_r.at[g, 1 + way], other))
+            )
+    for g in range(2):
+        far[g, 0].wait_recv()
+        far[g, 1].wait_recv()
+        across.append(start(pair(g, 2, core_s.at[g, 3], core_r.at[g, 3], other)))
+    for copy in across:
+        copy.wait_recv()
+    for copy in started:
+        copy.wait_send()
+
+
+def exchange_weights(out_weight):
+    depth, width = out_weight.shape
+    dma = pltpu.SemaphoreType.DMA
+    return pl.pallas_call(
+        weight_kernel,
+        out_shape=jax.ShapeDtypeStruct((4, depth, width // 8), out_weight.dtype),
+        in_specs=[pl.BlockSpec(memory_space=pl.ANY)],
+        out_specs=pl.BlockSpec(memory_space=pl.ANY),
+        scratch_shapes=[
+            dma((4,)), dma((4,)), dma((2, 2)), dma((2, 2)), dma((2, 2)), dma((2, 2)),
+            dma((2, 4)), dma((2, 4)),
+        ],
+        compiler_params=pltpu.CompilerParams(collective_id=1, has_side_effects=True),
+        name="weight_exchange",
+    )(out_weight)
+
+
+def project_kernel(
+    n_ref, w_ref, wr_ref, out_ref,
+    act, wts, mid, keep, direct, joined, own, relay, final,
+    load_s, act_s, y_s, y_r, mid_s, mid_r, fin_s, fin_r,
+):
+    z, y_lo, core, x, y_hi = place()
+    partner = device(z, y_lo, core, x, 1 - y_hi)
+    right = device(z, y_lo, core, (x + 1) % 4, y_hi)
+    left = device(z, y_lo, core, (x + 3) % 4, y_hi)
+    ways = (right, left)
+    tokens, depth = n_ref.shape
+    cols = out_ref.shape[1]
+    half = cols // 2
+    tiles = tokens // HALF
+
+    def rows(t):
+        return pl.ds(pl.multiple_of(t * HALF, HALF), HALF)
+
+    def loads(d):
+        block = 2 * ((x + REACH[d]) % 4) + y_hi
+        src = w_ref.at[:, pl.ds(pl.multiple_of(block * cols, cols), cols)]
+        return (
+            pltpu.make_async_copy(src, wts.at[d, pl.ds(0, depth)], load_s.at[d, 0]),
+            pltpu.make_async_copy(wr_ref.at[d], wts.at[d, pl.ds(depth, depth)], load_s.at[d, 1]),
+        )
+
+    own_act = pltpu.make_async_copy(n_ref, act.at[:, pl.ds(0, depth)], act_s)
+
+    def to_partner(t):
+        return remote(
+            n_ref.at[rows(t)], act.at[rows(t), pl.ds(depth, depth)], y_s.at[t], y_r.at[t], partner
+        )
+
+    def pass_on(t, way):
+        return remote(
+            mid.at[way, rows(t)], relay.at[way, rows(t)], mid_s.at[t, way], mid_r.at[t, way],
+            ways[way],
+        )
+
+    def send_direct(t, way):
+        return remote(
+            direct.at[way, rows(t)], final.at[way, 0, rows(t)], fin_s.at[t, way, 0],
+            fin_r.at[t, way, 0], ways[way],
+        )
+
+    def send_joined(t, way):
+        return remote(
+            joined.at[way, rows(t)], final.at[way, 1, rows(t)], fin_s.at[t, way, 1],
+            fin_r.at[t, way, 1], ways[way],
+        )
+
+    own_act.start()
+    for d in range(4):
+        for copy in loads(d):
+            copy.start()
+    greet([partner, right, left])
+    for t in range(tiles):
+        to_partner(t).start()
+    own_act.wait()
+
+    def product(t, d, side):
+        return jnp.dot(
+            act[rows(t)], wts[d, :, side * half : (side + 1) * half],
+            preferred_element_type=jnp.float32,
+        )
+
+    def ready(t, d):
+        @pl.when(t == 0)
+        def _():
+            for copy in loads(d):
+                copy.wait()
+
+    def finish(t):
+        for way in range(2):
+            send_direct(t, way).wait_recv()
+            send_joined(t, way).wait_recv()
+        r = rows(t)
+        for side in range(2):
+            total = own[r, side * half : (side + 1) * half]
+            total = total + final[0, 1 - side, r].astype(jnp.float32)
+            total = total + final[1, side, r].astype(jnp.float32)
+            out_ref[r, side * half : (side + 1) * half] = total.astype(out_ref.dtype)
+
+    def tile(t, carry):
+        r = rows(t)
+        to_partner(t).wait_recv()
+        ready(t, 0)
+        for way in range(2):
+            mid[way, r] = product(t, 0, way).astype(mid.dtype)
+            pass_on(t, way).start()
+        for way in range(2):
+            ready(t, 1 + way)
+            direct[way, r] = product(t, 1 + way, 1 - way).astype(direct.dtype)
+            send_direct(t, way).start()
+            keep[way, r] = product(t, 1 + way, way)
+        ready(t, 3)
+        for side in range(2):
+            own[r, side * half : (side + 1) * half] = product(t, 3, side)
+        for way in range(2):
+            pass_on(t, way).wait_recv()
+            joined[way, r] = (keep[way, r] + relay[way, r].astype(jnp.float32)).astype(joined.dtype)
+            send_joined(t, way).start()
+
+        @pl.when(t > 0)
+        def _():
+            finish(t - 1)
+
+        return carry
+
+    lax.fori_loop(0, tiles, tile, 0)
+    finish(tiles - 1)
+
+    def drain(t, carry):
+        to_partner(t).wait_send()
+        for way in range(2):
+            pass_on(t, way).wait_send()
+            send_direct(t, way).wait_send()
+            send_joined(t, way).wait_send()
+        return carry
+
+    lax.fori_loop(0, tiles, drain, 0)
+
+
+def project(normed, out_weight, received):
+    tokens, depth = normed.shape
+    cols = out_weight.shape[1] // 8
+    half = cols // 2
+    tiles = tokens // HALF
+    dma = pltpu.SemaphoreType.DMA
+    low, wide = jnp.bfloat16, jnp.float32
+    return pl.pallas_call(
+        project_kernel,
+        out_shape=jax.ShapeDtypeStruct((tokens, cols), low),
+        in_specs=[
+            pl.BlockSpec(memory_space=pltpu.VMEM),
+            pl.BlockSpec(memory_space=pl.ANY),
+            pl.BlockSpec(memory_space=pl.ANY),
+        ],
+        out_specs=pl.BlockSpec(memory_space=pltpu.VMEM),
+        scratch_shapes=[
+            pltpu.VMEM((tokens, 2 * depth), low),
+            pltpu.VMEM((4, 2 * depth, cols), low),
+            pltpu.VMEM((2, tokens, half), low),
+            pltpu.VMEM((2, tokens, half), wide),
+            pltpu.VMEM((2, tokens, half), low),
+            pltpu.VMEM((2, tokens, half), low),
+            pltpu.VMEM((tokens, cols), wide),
+            pltpu.VMEM((2, tokens, half), low),
+            pltpu.VMEM((2, 2, tokens, half), low),
+            dma((4, 2)), dma, dma((tiles,)), dma((tiles,)), dma((tiles, 2)), dma((tiles, 2)),
+            dma((tiles, 2, 2)), dma((tiles, 2, 2)),
+        ],
+        compiler_params=pltpu.CompilerParams(
+            collective_id=2, has_side_effects=True, vmem_limit_bytes=56 << 20
+        ),
+        name="projection",
+    )(normed, out_weight, received)
 
 
 def shifted(block, axis, distance):
@@ -124,15 +392,8 @@
     normed = (
         (grouped * lax.rsqrt(spread + 1e-05)).reshape(seq_count * tok_count, inner_cols) * norm_gain
     ).astype(jnp.bfloat16)
-    summed_out = lax.psum_scatter(
-        lax.dot_general(
-            out_weight, normed, (((0,), (1,)), ((), ())), preferred_element_type=jnp.float32
-        ).astype(jnp.bfloat16),
-        "head",
-        scatter_dimension=0,
-        tiled=True,
-    ).astype(jnp.float32)
-    return summed_out.T.reshape(seq_count, tok_count, summed_out.shape[0]).astype(jnp.bfloat16)
+    projected = project(normed, out_weight, exchange_weights(out_weight))
+    return projected.reshape(seq_count, tok_count, projected.shape[1])
 
 
 def body(x_in, z_in, bc_in, conv_x, conv_bc, dt_raw, a_log, skip_scale, norm_gain, out_weight):

time: 300 us -> 225 us (0.75)
  waiting for transfers between devices: 179 us -> 19 us
  Pallas kernels: 0 us -> 125 us
  matrix products: 30.5 us -> 9.22 us
  between operations: 13.8 us -> 0.35 us
  other arithmetic: 29.8 us -> 23.9 us
    reduce_scatter x1 -> x0, waiting for transfers between devices: 150 us -> none  [mixer(): lax.psum_scatter(lax.dot_general(out_weight, normed, (((0,), (1,)), ((),...]
    pallas_call x0 -> x2, Pallas kernels: none -> 125 us  [the longest x1 69.2 us: project(): pl.pallas_call(project_kernel, out_shape=jax.ShapeDtypeStruct((tokens, co...]
    dot_general x1 -> x0, matrix products: 21.8 us -> none  [mixer(): lax.dot_general(out_weight, normed, (((0,), (1,)), ((), ())), preferred_e...]
    all_to_all x1, waiting for transfers between devices: 11 us -> 0.01 us  [chain_entries(): back = lax.all_to_all(stacked, 'ctx', 0, 0)]
    reshape x1 -> x2, local copies, waits for them, and re-layouts: 5.45 us -> 11.4 us  [mixer(): ssm_out.reshape(seq_count, tok_count, inner_cols)]
    add x1 -> x0, local copies, waits for them, and re-layouts: 4.73 us -> none  [mixer(): ssm_out = intra_part + carried + skip_scale[None, None, :, None] * xs_all]
    convert_element_type x16, other arithmetic: 5.12 us -> 1.07 us  [chain_entries(): entry[c][half] = state.astype(jnp.bfloat16)]
    reduce_sum x1, other arithmetic: 5.64 us -> 2.54 us  [mixer(): spread = jnp.mean(grouped * grouped, axis=3, keepdims=True)]
  transfers between devices with their start and end apart: 6 -> 5, of which waited for: 5 -> 3; matrix products, arithmetic and copies ran while one was open for 6% -> 6% of each run, Pallas kernels for 0% -> 25%
where the time goes in v2:
time: 225 us; the launch traced here: 223 us
  Pallas kernels  125 us (56%)
  other arithmetic  23.9 us (11%)
  starting transfers between devices  23.3 us (10%)
  local copies, waits for them, and re-layouts  22.4 us (10%)
  waiting for transfers between devices  19 us (8%)
  matrix products  9.22 us (4%)
    pallas_call x1, Pallas kernels, project(): pl.pallas_call(project_kernel, out_shape=jax.ShapeDtypeStruct((tokens, co...  69.2 us
    pallas_call x1, Pallas kernels, exchange_weights(): pl.pallas_call(weight_kernel, out_shape=jax.ShapeDtypeStruct((4, depth, w...  55.8 us
    all_to_all x2, starting transfers between devices, spread(): return lax.all_to_all(jnp.moveaxis(split, 2, 0), 'ctx', 0, 0)  15.1 us
    all_to_all x2, waiting for transfers between devices, spread(): return lax.all_to_all(jnp.moveaxis(split, 2, 0), 'ctx', 0, 0)  15 us
    reshape x2, local copies, waits for them, and re-layouts, mixer(): ssm_out.reshape(seq_count, tok_count, inner_cols)  11.4 us
    unnamed x14, other arithmetic  8.87 us
    dot_general x1, matrix products, mixer(): jnp.einsum('bhqu,buhp->bqhp', weights, xs_all, preferred_element_type=jnp...  5.93 us
  transfers between devices with their start and end apart: 5, of which 3 were waited for; matrix products, arithmetic and copies ran while one was open for 6% of the time, Pallas kernels for 25%

profile of v2, /device:TPU:1, one launch (start us, length us, event | category | flops | bytes accessed | tf_op | source)
XLA Modules:
  0.0 223.2 jit_solution(4017483410393449021)
XLA Ops:
  1.8 2.3 %reduce-window.6 = f32[4,16,2,128]{3,1,2,0:T(8,128)S(1)} reduce-window(f32[4,16,2,128]{3,1,2,0:T(8,128)S(1)} %copy_bitcast_fusion.2, f32[]{:T(128)} %constant.7.clone.1), window={size=1x1x1x128 pad=0_0x0_0x0_0x127_0}, to_apply=%region_0.1 | reduce-window | flops 2080768 | bytes 131076 | tf_op jit(solution)/shard_map/reduce-window
  5.3 7.8 %all-to-all-start = ((f32[16,2,2,1]{2,1,3,0:T(2,128)}), f32[16,2,2,1]{2,1,3,0:T(2,128)S(1)}, u32[]{:S(2)}, u32[]{:S(2)}) async-start(f32[16,2,2,1]{2,1,3,0:T(2,128)} %copy.199), calls=%async_computation | async-start | bytes 32768 | tf_op jit(solution)/shard_map/all_to_all | solution.py:297
  13.1 1.2 concatenate.19
  15.1 2.0 collective-permute-start.1
  17.3 2.9 %collective-permute-done.1 = bf16[2,3,1280]{2,1,0:T(4,128)(2,1)S(1)} collective-permute-done((bf16[2,3,1280]{2,1,0:T(4,128)(2,1)S(1)}, bf16[2,3,1280]{2,1,0:T(4,128)(2,1)S(1)}, u32[]{:S(2)}, u32[]{:S(2)}) %collective-permute-start.1) | collective-permute-done | bytes 15392 | tf_op jit(solution)/shard_map/ppermute | solution.py:283
  20.3 1.9 collective-permute-start
  22.3 1.1 collective-permute-done
  23.9 2.4 %divide_convert_fusion = bf16[2,2,192,1280]{3,2,1,0:T(8,128)(2,1)S(1)} fusion(bf16[2,2,192,256]{3,2,1,0:T(8,128)(2,1)S(1)} %concatenate.19, bf16[2,2,195,1280]{3,2,1,0:T(8,128)(2,1)S(1)} %maximum_maximum_fusion, f32[1280]{0:T(1024)S(1)} %get-tuple-element.8, f32[1280]{0:T(1024)S(1)} %get-tuple-element.9, f32[1280]{0:T(1024)S(1)} %get-tuple-element.10, ...), kind=kLoop, calls=%fused_computation.16 | loop fusion | flops 17694720 | bytes 9850880 | tf_op jit(solution)/shard_map/convert_element_type | solution.py:340
  26.6 2.5 %copy.194 = bf16[2,2,192,1024]{2,3,1,0:T(8,128)(2,1)} copy(bf16[2,2,192,1024]{3,2,1,0:T(8,128)(2,1)S(1)} %slice.337) | data formatting | bytes 3145728 | tf_op jit(solution)/shard_map/slice | solution.py:341
  29.1 2.3 %fusion.17 = bf16[4,16,64,128]{3,2,1,0:T(8,128)(2,1)S(1)} fusion(bf16[4,192,128,1]{2,1,3,0:T(8,128)(2,1)S(1)} %bitcast.435, bf16[4,192,16,64]{1,3,2,0:T(8,128)(2,1)} %bitcast.430, f32[4,192,16]{1,2,0:T(8,128)S(1)} %get-tuple-element.89), kind=kOutput, calls=%fused_computation.32 | convolution fusion | flops 204210176 | bytes 2867200 | tf_op jit(solution)/shard_map/bugkp,bugn->bgkpn/dot_general | solution.py:367
  31.4 1.0 copy.278
  32.5 7.2 %all-to-all-start.1 = ((bf16[16,2,2,1,64,128]{5,4,2,1,3,0:T(8,128)(2,1)}), bf16[16,2,2,1,64,128]{5,4,2,1,3,0:T(8,128)(2,1)S(1)}, u32[]{:S(2)}, u32[]{:S(2)}) async-start(bf16[16,2,2,1,64,128]{5,4,2,1,3,0:T(8,128)(2,1)} %bitcast.422), calls=%async_computation.1 | async-start | bytes 2097152 | tf_op jit(solution)/shard_map/all_to_all | solution.py:297
  40.5 15.0 %all-to-all-done.1 = bf16[16,2,2,1,64,128]{5,4,2,1,3,0:T(8,128)(2,1)S(1)} async-done(((bf16[16,2,2,1,64,128]{5,4,2,1,3,0:T(8,128)(2,1)}), bf16[16,2,2,1,64,128]{5,4,2,1,3,0:T(8,128)(2,1)S(1)}, u32[]{:S(2)}, u32[]{:S(2)}) %all-to-all-start.1) | async-done | bytes 1048608 | tf_op jit(solution)/shard_map/all_to_all | solution.py:297
  66.8 4.3 %all-to-all-start.2 = ((bf16[16,2,2,1,64,128]{5,4,1,2,3,0:T(8,128)(2,1)}), bf16[16,2,2,1,64,128]{5,4,1,2,3,0:T(8,128)(2,1)S(1)}, u32[]{:S(2)}, u32[]{:S(2)}) async-start(bf16[16,2,2,1,64,128]{5,4,1,2,3,0:T(8,128)(2,1)} %fusion.34), calls=%async_computation.2 | async-start | bytes 2097152 | tf_op jit(solution)/shard_map/all_to_all | solution.py:310
  71.1 55.8 %weight_exchange.1.wr_ref = bf16[4,1024,1024]{2,1,0:T(8,128)(2,1)} custom-call(bf16[1024,8192]{1,0:T(8,128)(2,1)} %w_ref.3), custom_call_target="tpu_custom_call" | custom-call | tf_op jit(solution)/shard_map/weight_exchange/pallas_call | solution.py:107
  128.1 0.8 copy-done.2
  128.9 5.9 %fusion.8 = f32[4,192,16,64]{1,3,2,0:T(8,128)} fusion(bf16[4,192,16,64]{1,3,2,0:T(8,128)(2,1)S(1)} %bitcast.431, f32[4,16,64,192]{3,2,1,0:T(8,128)S(1)} %fusion.73, f32[4,16,192]{2,1,0:T(8,128)S(1)} %bitcast.439, f32[4,16,192]{2,1,0:T(8,128)S(1)} %get-tuple-element.90, f32[4,192,192]{2,1,0:T(8,128)S(1)} %fusion.72, ...), kind=kOutput, calls=%fused_computation.11 | convolution fusion | flops 320077824 | bytes 8638528 | tf_op jit(solution)/shard_map/bhqu,buhp->bqhp/dot_general | solution.py:364
  134.8 6.6 %copy.237 = f32[4,192,16,64]{3,2,1,0:T(8,128)} copy(f32[4,192,16,64]{1,3,2,0:T(8,128)} %fusion.8) | data formatting | bytes 6291456 | tf_op jit(solution)/shard_map/reshape | solution.py:387
  141.5 4.8 %reshape.3426 = f32[2,384,1024]{2,1,0:T(8,128)S(1)} reshape(f32[4,192,16,64]{3,2,1,0:T(8,128)} %copy.237) | data formatting | bytes 6291456 | tf_op jit(solution)/shard_map/reshape | solution.py:387
  146.3 2.5 %multiply_reduce_fusion = f32[2,384]{1,0:T(2,128)S(1)} fusion(f32[2,384,1024]{2,1,0:T(8,128)S(1)} %reshape.3426, bf16[2,384,1024]{2,1,0:T(8,128)(2,1)} %param.11), kind=kLoop, calls=%fused_computation.22 | loop fusion | flops 5504256 | bytes 4721664 | tf_op jit(solution)/shard_map/reduce_sum | solution.py:391
  148.9 0.9 broadcast_multiply_fusion
  149.8 1.6 fusion.13.n_ref
  151.3 69.2 %projection.1 = bf16[768,1024]{1,0:T(8,128)(2,1)} custom-call(bf16[768,1024]{1,0:T(8,128)(2,1)} %fusion.13.n_ref, bf16[1024,8192]{1,0:T(8,128)(2,1)} %w_ref.3, bf16[4,1024,1024]{2,1,0:T(8,128)(2,1)} %weight_exchange.1.wr_ref), custom_call_target="tpu_custom_call" | custom-call | tf_op jit(solution)/shard_map/projection/pallas_call | solution.py:251
  220.5 2.7 %copy.296 = bf16[2,384,1024]{2,1,0:T(8,128)(2,1)} copy(bf16[2,384,1024]{2,1,0:T(8,128)(2,1)} %bitcast.427) | data formatting | bytes 3145728
  (77 shorter events, 17.9 us)
Async XLA Ops:
  0.0 20.3 %copy-start = (bf16[2,384,1024]{2,1,0:T(8,128)(2,1)S(1)}, bf16[2,384,1024]{2,1,0:T(8,128)(2,1)}, u32[]{:S(2)}) copy-start(bf16[2,384,1024]{2,1,0:T(8,128)(2,1)} %param.10) | copy-start | bytes 4718596
  0.0 17.2 %copy-start.3 = (f32[4,1024]{1,0:T(4,128)S(1)}, f32[4,1024]{1,0:T(4,128)}, u32[]{:S(2)}) copy-start(f32[4,1024]{1,0:T(4,128)} %param.13) | copy-start | bytes 49156
  0.0 17.3 %copy-start.4 = (f32[4,2,128]{2,1,0:T(2,128)S(1)}, f32[4,2,128]{2,1,0:T(2,128)}, u32[]{:S(2)}) copy-start(f32[4,2,128]{2,1,0:T(2,128)} %param.14) | copy-start | bytes 12292
  5.3 27.2 %all-to-all-start = ((f32[16,2,2,1]{2,1,3,0:T(2,128)}), f32[16,2,2,1]{2,1,3,0:T(2,128)S(1)}, u32[]{:S(2)}, u32[]{:S(2)}) async-start(f32[16,2,2,1]{2,1,3,0:T(2,128)} %copy.199), calls=%async_computation | async-start | bytes 32768 | tf_op jit(solution)/shard_map/all_to_all | solution.py:297
  15.1 5.1 %collective-permute-start.1 = (bf16[2,3,1280]{2,1,0:T(4,128)(2,1)S(1)}, bf16[2,3,1280]{2,1,0:T(4,128)(2,1)S(1)}, u32[]{:S(2)}, u32[]{:S(2)}) collective-permute-start(bf16[2,3,1280]{2,1,0:T(4,128)(2,1)S(1)} %fusion.55), channel_id=1, source_target_pairs={{8,0},{16,8},{24,16},{32,24},{40,32},{48,40},{56,48},{64,56},{72,6... | collective-permute-start | bytes 46088 | tf_op jit(solution)/shard_map/ppermute | solution.py:283
  20.3 3.1 %collective-permute-start = (bf16[2,3,1280]{2,1,0:T(4,128)(2,1)S(1)}, bf16[2,3,1280]{2,1,0:T(4,128)(2,1)S(1)}, u32[]{:S(2)}, u32[]{:S(2)}) collective-permute-start(bf16[2,3,1280]{2,1,0:T(4,128)(2,1)S(1)} %get-tuple-element.65), channel_id=1, source_target_pairs={{0,8},{8,16},{16,24},{24,32},{32,40},{40,48},{48,56},{56,64},{64,7... | collective-permute-start | bytes 46088 | tf_op jit(solution)/shard_map/ppermute | solution.py:283
  32.5 23.1 %all-to-all-start.1 = ((bf16[16,2,2,1,64,128]{5,4,2,1,3,0:T(8,128)(2,1)}), bf16[16,2,2,1,64,128]{5,4,2,1,3,0:T(8,128)(2,1)S(1)}, u32[]{:S(2)}, u32[]{:S(2)}) async-start(bf16[16,2,2,1,64,128]{5,4,2,1,3,0:T(8,128)(2,1)} %bitcast.422), calls=%async_computation.1 | async-start | bytes 2097152 | tf_op jit(solution)/shard_map/all_to_all | solution.py:297
  66.8 60.4 %all-to-all-start.2 = ((bf16[16,2,2,1,64,128]{5,4,1,2,3,0:T(8,128)(2,1)}), bf16[16,2,2,1,64,128]{5,4,1,2,3,0:T(8,128)(2,1)S(1)}, u32[]{:S(2)}, u32[]{:S(2)}) async-start(bf16[16,2,2,1,64,128]{5,4,1,2,3,0:T(8,128)(2,1)} %fusion.34), calls=%async_computation.2 | async-start | bytes 2097152 | tf_op jit(solution)/shard_map/all_to_all | solution.py:310
  127.3 1.6 copy-start.2
  127.3 1.6 copy-start.6
  146.3 2.6 %copy-start.1 = (bf16[2,384,1024]{2,1,0:T(8,128)(2,1)S(1)}, bf16[2,384,1024]{2,1,0:T(8,128)(2,1)}, u32[]{:S(2)}) copy-start(bf16[2,384,1024]{2,1,0:T(8,128)(2,1)} %param.11) | copy-start | bytes 4718596
  148.9 0.9 copy-start.5

commit v3 on v2

v3 whole, which is shorter than its diff:
```python
import jax
import jax.numpy as jnp
from jax import lax
from jax.experimental import pallas as pl
from jax.experimental.pallas import tpu as pltpu
from jax.sharding import PartitionSpec as P

HEAD_DIM = 64
STATE = 128
KW = 4
HALF = 192
MESH = pl.DeviceIdType.MESH
REACH = (2, 1, 3, 0)


def place():
    c, h = lax.axis_index("ctx"), lax.axis_index("head")
    return c // 4, (c // 2) % 2, c % 2, h // 2, h % 2


def device(z, y_lo, core, x, y_hi):
    return (z * 4 + y_lo * 2 + core, x * 2 + y_hi)


def greet(devices):
    barrier = pltpu.get_barrier_semaphore()
    for one in devices:
        pl.semaphore_signal(barrier, inc=1, device_id=one, device_id_type=MESH)
    pl.semaphore_wait(barrier, len(devices))


def remote(src, dst, send_sem, recv_sem, target):
    return pltpu.make_async_remote_copy(
        src_ref=src,
        dst_ref=dst,
        send_sem=send_sem,
        recv_sem=recv_sem,
        device_id=target,
        device_id_type=MESH,
    )


def rounded_parts(values):
    high = values.astype(jnp.bfloat16)
    rest = values - high.astype(jnp.float32)
    middle = rest.astype(jnp.bfloat16)
    low = (rest - middle.astype(jnp.float32)).astype(jnp.bfloat16)
    return jnp.concatenate([high, middle, low], axis=0)


def unit(size):
    rows = lax.broadcasted_iota(jnp.int32, (size, size), 0)
    cols = lax.broadcasted_iota(jnp.int32, (size, size), 1)
    return jnp.where(rows == cols, 1.0, 0.0).astype(jnp.bfloat16)


def by_rows(left, right):
    return lax.dot_general(
        left, right, (((1,), (1,)), ((), ())), preferred_element_type=jnp.float32
    )


def mixer_kernel(
    x_ref, bc_ref, dt_ref, a_ref, skip_ref, gain_ref, taps_ref, taps_bc_ref, z_ref, w_ref,
    n_ref, wr_ref,
    halo_x, halo_bc, wide, xs, bs, cs, cum_row, dt_row, cum_col, tail3, cum3, spread3,
    scaled, upd, got, back, ent, dec, decs, steps, inner, zbuf,
    z_sem, halo_s, halo_r, dec_s, dec_r, own_s, upd_s, upd_r, ent_s, ent_r,
    in_s, in_r, z_s, z_r, far_s, far_r, core_s, core_r,
):
    f32, bf16 = jnp.float32, jnp.bfloat16
    z, y_lo, core, x, y_hi = place()
    me = lax.axis_index("ctx")
    head = lax.axis_index("head")
    cols = x_ref.shape[3]
    state_rows, lanes = got.shape[2:]
    heads = dt_ref.shape[1]

    partner = device(z, 1 - y_lo, core, x, 1 - y_hi)
    up = device((z + 1) % 4, y_lo, core, x, y_hi)
    down = device((z + 3) % 4, y_lo, core, x, y_hi)
    other = device(z, y_lo, 1 - core, x, y_hi)
    depth = wr_ref.shape[1]
    part = depth // 8

    def part_rows(step):
        return pl.ds(pl.multiple_of((((z + step) % 4) * 2 + core) * part, part), part)

    def import_part(d):
        block = 2 * ((x + REACH[d]) % 4) + 1 - y_hi
        src = w_ref.at[part_rows(0), pl.ds(pl.multiple_of(block * cols, cols), cols)]
        return remote(src, wr_ref.at[d, part_rows(0)], in_s.at[d], in_r.at[d], partner)

    def near(g, way):
        here = wr_ref.at[pl.ds(2 * g, 2), part_rows(0)]
        return remote(here, here, z_s.at[g, way], z_r.at[g, way], down if way else up)

    def far(g, way):
        here = wr_ref.at[2 * g + way, part_rows(1 if way else 3)]
        return remote(here, here, far_s.at[g, way], far_r.at[g, way], down if way else up)

    def across(g, step):
        here = wr_ref.at[pl.ds(2 * g, 2), part_rows(step)]
        return remote(here, here, core_s.at[g, step], core_r.at[g, step], other)

    def weights_first(g):
        import_part(2 * g).wait_recv()
        import_part(2 * g + 1).wait_recv()
        near(g, 0).start()
        near(g, 1).start()
        across(g, 0).start()

    def weights_second(g):
        for way in range(2):
            near(g, way).wait_recv()
            far(g, way).start()
            across(g, 1 if way else 3).start()

    def weights_third(g):
        far(g, 0).wait_recv()
        far(g, 1).wait_recv()
        across(g, 2).start()

    def weights_end():
        for g in range(2):
            for step in range(4):
                across(g, step).wait_recv()
        for d in range(4):
            import_part(d).wait_send()
        for g in range(2):
            for way in range(2):
                near(g, way).wait_send()
                far(g, way).wait_send()
            for step in range(4):
                across(g, step).wait_send()

    def peer(step):
        return (me + step) % 16

    def at(index):
        return (index, head)

    def halo(half):
        target = at(peer(15 if half else 1))
        rows = pl.ds(HALF - 16, 16)
        return (
            remote(
                x_ref.at[:, half, rows], halo_x.at[half], halo_s.at[half, 0], halo_r.at[half, 0],
                target,
            ),
            remote(
                bc_ref.at[:, half, rows], halo_bc.at[half], halo_s.at[half, 1],
                halo_r.at[half, 1], target,
            ),
        )

    def share(ref, s, owner):
        return ref.at[
            pl.ds(2 * s, 2),
            pl.ds(pl.multiple_of((owner // 2) * state_rows, state_rows), state_rows),
            pl.ds(pl.multiple_of((owner % 2) * lanes, lanes), lanes),
        ]

    def send_decay(step):
        return remote(dec, decs.at[me], dec_s.at[step], dec_r.at[step], at(peer(step)))

    def send_update(s, step):
        owner = peer(step)
        return remote(
            share(upd, s, owner), got.at[me, pl.ds(2 * s, 2)], upd_s.at[s, step],
            upd_r.at[s, step], at(owner),
        )

    def send_entry(s, step):
        target = peer(step)
        return remote(
            back.at[target, pl.ds(2 * s, 2)], share(ent, s, me), ent_s.at[s, step],
            ent_r.at[s, step], at(target),
        )

    def keep_update(s):
        return pltpu.make_async_copy(share(upd, s, me), got.at[me, pl.ds(2 * s, 2)], own_s.at[s])

    def keep_entry(s):
        return pltpu.make_async_copy(back.at[me, pl.ds(2 * s, 2)], share(ent, s, me), own_s.at[s])

    def each_peer(work):
        def step(i, carry):
            work(i)
            return carry

        lax.fori_loop(1, 16, step, 0)

    z_copy = pltpu.make_async_copy(z_ref, zbuf, z_sem)
    z_copy.start()
    barrier = pltpu.get_barrier_semaphore()

    def hello(i):
        pl.semaphore_signal(barrier, inc=1, device_id=at(peer(i)), device_id_type=MESH)

    each_peer(hello)
    pl.semaphore_signal(barrier, inc=1, device_id=partner, device_id_type=MESH)
    pl.semaphore_wait(barrier, 16)
    for half in range(2):
        for copy in halo(half):
            copy.start()
    for d in range(4):
        import_part(d).start()

    row_id = lax.broadcasted_iota(jnp.int32, (HALF, HALF), 0)
    col_id = lax.broadcasted_iota(jnp.int32, (HALF, HALF), 1)
    causal = row_id >= col_id
    eye = unit(HALF)
    ahead = jnp.where(row_id <= col_id, 1.0, 0.0).astype(bf16)
    rate = -jnp.exp(a_ref[...])
    dec[...] = jnp.zeros_like(dec)
    for b in range(4):
        raw = dt_ref[b]
        step_size = jnp.maximum(raw, 0.0) + jnp.log1p(jnp.exp(-jnp.abs(raw)))
        fall = rounded_parts(step_size * rate)
        sums = jnp.dot(fall, ahead, preferred_element_type=f32)
        cum = sums[:heads] + sums[heads : 2 * heads] + sums[2 * heads :]
        dt_row[b] = step_size
        cum_row[b] = cum
        turned = by_rows(eye, rounded_parts(cum))
        col = turned[:, :heads] + turned[:, heads : 2 * heads] + turned[:, 2 * heads :]
        cum_col[b] = col
        dec[b : b + 1, :heads] = jnp.exp(col[HALF - 1 :])
        tail = jnp.exp(cum[:, HALF - 1 :] - cum) * step_size
        tail3[b] = by_rows(eye, rounded_parts(tail)).astype(bf16)
        cum3[b] = by_rows(eye, rounded_parts(jnp.exp(cum))).astype(bf16)
    of_head = lax.broadcasted_iota(jnp.int32, spread3.shape, 1) // HEAD_DIM
    of_part = lax.broadcasted_iota(jnp.int32, spread3.shape, 0) % heads
    spread3[...] = jnp.where(of_head == of_part, 1.0, 0.0).astype(bf16)
    each_peer(lambda i: send_decay(i).start())
    decs[me] = dec[...]
    for half in range(2):
        for copy in halo(half):
            copy.wait_recv()

    turn = unit(STATE)
    chunk = 256
    band = 64

    def convolve(s, half, start, width, src, lead_ref, taps, put):
        before = lead_ref[0, s, :, pl.ds(start, width)]
        before = jnp.where(me == 0, jnp.zeros_like(before), before)
        turned = jnp.where(
            me == 15, src[s, 0, HALF - 16 :, pl.ds(start, width)],
            lead_ref[1, s, :, pl.ds(start, width)],
        )
        lead = jnp.where(half == 0, before, turned)
        wide[0:8] = lead.astype(f32)[8:]
        wide[8:] = src[s, half, :, pl.ds(start, width)].astype(f32)
        tap = taps[:, pl.ds(start, width)]
        for r in range(0, HALF, band):
            total = tap[0:1] * wide[r + 5 : r + 5 + band]
            for k in range(1, KW):
                total = total + tap[k : k + 1] * wide[r + 5 + k : r + 5 + k + band]
            put(r, (total / (1.0 + jnp.exp(-total))).astype(bf16))

    def front(b, carry):
        s, half = b // 2, b % 2

        def put_bc(r, values):
            bs[b, r : r + band] = values[:, :STATE]
            cs[b, r : r + band] = values[:, STATE:]

        convolve(s, half, 0, chunk, bc_ref, halo_bc, taps_bc_ref, put_bc)
        bs_turned = by_rows(turn, bs[b]).astype(bf16)

        def columns(i, carry):
            start = pl.multiple_of(i * chunk, chunk)

            def put(r, values):
                xs[b, r : r + band, pl.ds(start, chunk)] = values

            convolve(s, half, start, chunk, x_ref, halo_x, taps_ref, put)
            for r in range(0, HALF, band):
                factor = jnp.dot(
                    tail3[b, r : r + band], spread3[:, pl.ds(start, chunk)],
                    preferred_element_type=f32,
                )
                scaled[r : r + band] = (
                    factor * xs[b, r : r + band, pl.ds(start, chunk)].astype(f32)
                ).astype(bf16)
            upd[b, :, pl.ds(start, chunk)] = jnp.dot(
                bs_turned, scaled[...], preferred_element_type=f32
            ).astype(bf16)
            return carry

        lax.fori_loop(0, cols // chunk, columns, 0)

        @pl.when(half == 1)
        def _():
            each_peer(lambda i: send_update(s, i).start())
            keep_update(s).start()

        return carry

    lax.fori_loop(0, 4, front, 0)

    first = 128

    def intra(b, carry):
        scores = jnp.where(causal, by_rows(cs[b], bs[b]), 0.0)
        low_half = lax.broadcasted_iota(jnp.int32, (1, 128), 1) < HEAD_DIM
        for p in range(heads // 2):
            tops, ends = [], []
            for h in (2 * p, 2 * p + 1):
                col = cum_col[b, :, h : h + 1]
                row = cum_row[b, h : h + 1]
                size = dt_row[b, h : h + 1]
                gap = jnp.minimum(col[:first] - row[:, :first], 0.0)
                tops.append(
                    (scores[:first, :first] * jnp.exp(gap) * size[:, :first]).astype(bf16)
                )
                gap = jnp.minimum(col[first:] - row, 0.0)
                ends.append((scores[first:] * jnp.exp(gap) * size).astype(bf16))
            pair = slice(128 * p, 128 * p + 128)
            top = jnp.dot(
                jnp.concatenate(tops, axis=0), xs[b, :first, pair], preferred_element_type=f32
            )
            end = jnp.dot(
                jnp.concatenate(ends, axis=0), xs[b, :, pair], preferred_element_type=f32
            )
            inner[b, :first, pair] = jnp.where(low_half, top[:first], top[first:])
            rest = HALF - first
            inner[b, first:, pair] = jnp.where(low_half, end[:rest], end[rest:])
        return carry

    def chain(s):
        each_peer(lambda i: send_update(s, i).wait_recv())
        keep_update(s).wait()
        state = jnp.zeros((state_rows, lanes), f32)
        for i in range(32):
            c, half = (i, 0) if i < 16 else (31 - i, 1)
            b = 2 * s + half
            back[c, b] = state.astype(bf16)
            state = steps[8 * c + b : 8 * c + b + 1] * state + got[c, b].astype(f32)
        each_peer(lambda i: send_entry(s, i).start())
        keep_entry(s).start()

    def finish(b, carry):
        squares = [jnp.zeros((96, 128), f32)] * 2
        for q in range(cols // chunk):
            part_cols = slice(q * chunk, (q + 1) * chunk)
            for i in range(2):
                r = slice(96 * i, 96 * i + 96)
                carried = jnp.dot(cs[b, r], ent[b, :, part_cols], preferred_element_type=f32)
                factor = jnp.dot(cum3[b, r], spread3[:, part_cols], preferred_element_type=f32)
                total = inner[b, r, part_cols] + factor * carried
                total = total + skip_ref[:, part_cols] * xs[b, r, part_cols].astype(f32)
                gate = zbuf[b, r, part_cols].astype(f32)
                total = total * (gate / (1.0 + jnp.exp(-gate)))
                inner[b, r, part_cols] = total
                square = total * total
                squares[i] = squares[i] + square[:, :128] + square[:, 128:]
        for i in range(2):
            spread = jnp.sum(squares[i], axis=1, keepdims=True) * (1.0 / cols)
            scale = lax.rsqrt(spread + 1e-05)
            r = slice(96 * i, 96 * i + 96)
            for q in range(cols // chunk):
                part_cols = slice(q * chunk, (q + 1) * chunk)
                n_ref[b, r, part_cols] = (
                    inner[b, r, part_cols] * scale * gain_ref[:, part_cols]
                ).astype(bf16)
        return carry

    def enter(s):
        each_peer(lambda i: send_entry(s, i).wait_recv())
        keep_entry(s).wait()

    weights_first(0)
    lax.fori_loop(0, 2, intra, 0)
    each_peer(lambda i: send_decay(i).wait_recv())
    head_id = lax.broadcasted_iota(jnp.int32, (128, lanes), 0)
    lane_head = lax.broadcasted_iota(jnp.int32, (128, lanes), 1) // HEAD_DIM
    picks = jnp.where(head_id == lane_head + (me % 2) * (lanes // HEAD_DIM), 1.0, 0.0).astype(bf16)
    stacked = rounded_parts(decs[...].reshape(128, 128))
    parts = jnp.dot(stacked, picks, preferred_element_type=f32)
    steps[...] = parts[:128] + parts[128:256] + parts[256:]
    chain(0)
    weights_first(1)
    lax.fori_loop(2, 4, intra, 0)
    chain(1)
    weights_second(0)
    z_copy.wait()
    enter(0)
    lax.fori_loop(0, 2, finish, 0)
    weights_second(1)
    weights_third(0)
    enter(1)
    lax.fori_loop(2, 4, finish, 0)
    weights_third(1)

    for half in range(2):
        for copy in halo(half):
            copy.wait_send()

    def drain(i):
        send_decay(i).wait_send()
        for s in range(2):
            send_update(s, i).wait_send()
            send_entry(s, i).wait_send()

    each_peer(drain)
    weights_end()


def mix(x_part, bc_part, dt_part, a_log, skip_scale, norm_gain, conv_x, conv_bc, z_part, weight):
    blocks, heads = dt_part.shape[:2]
    cols = x_part.shape[3]
    depth, width = weight.shape
    dma = pltpu.SemaphoreType.DMA
    low, wide = jnp.bfloat16, jnp.float32
    vmem = pl.BlockSpec(memory_space=pltpu.VMEM)
    hbm = pl.BlockSpec(memory_space=pl.ANY)
    return pl.pallas_call(
        mixer_kernel,
        out_shape=(
            jax.ShapeDtypeStruct((blocks, HALF, cols), low),
            jax.ShapeDtypeStruct((4, depth, width // 8), low),
        ),
        in_specs=[vmem] * 8 + [hbm] * 2,
        out_specs=(vmem, hbm),
        scratch_shapes=[
            pltpu.VMEM((2, 2, 16, cols), low),
            pltpu.VMEM((2, 2, 16, 2 * STATE), low),
            pltpu.VMEM((8 + HALF, 256), wide),
            pltpu.VMEM((blocks, HALF, cols), low),
            pltpu.VMEM((blocks, HALF, STATE), low),
            pltpu.VMEM((blocks, HALF, STATE), low),
            pltpu.VMEM((blocks, heads, HALF), wide),
            pltpu.VMEM((blocks, heads, HALF), wide),
            pltpu.VMEM((blocks, HALF, heads), wide),
            pltpu.VMEM((blocks, HALF, 3 * heads), low),
            pltpu.VMEM((blocks, HALF, 3 * heads), low),
            pltpu.VMEM((3 * heads, cols), low),
            pltpu.VMEM((HALF, 256), low),
            pltpu.VMEM((blocks, STATE, cols), low),
            pltpu.VMEM((16, blocks, STATE // 8, cols // 2), low),
            pltpu.VMEM((16, blocks, STATE // 8, cols // 2), low),
            pltpu.VMEM((blocks, STATE, cols), low),
            pltpu.VMEM((8, 128), wide),
            pltpu.VMEM((16, 8, 128), wide),
            pltpu.VMEM((128, cols // 2), wide),
            pltpu.VMEM((blocks, HALF, cols), wide),
            pltpu.VMEM((blocks, HALF, cols), low),
            dma, dma((2, 2)), dma((2, 2)), dma((16,)), dma((16,)), dma((2,)),
            dma((2, 16)), dma((2, 16)), dma((2, 16)), dma((2, 16)),
            dma((4,)), dma((4,)), dma((2, 2)), dma((2, 2)), dma((2, 2)), dma((2, 2)),
            dma((2, 4)), dma((2, 4)),
        ],
        compiler_params=pltpu.CompilerParams(
            collective_id=1, has_side_effects=True, vmem_limit_bytes=56 << 20
        ),
        name="mixer",
    )(x_part, bc_part, dt_part, a_log, skip_scale, norm_gain, conv_x, conv_bc, z_part, weight)


def project_kernel(
    n_ref, w_ref, wr_ref, out_ref,
    act, wts, mid, keep, direct, joined, own, relay, final,
    load_s, act_s, y_s, y_r, mid_s, mid_r, fin_s, fin_r,
):
    z, y_lo, core, x, y_hi = place()
    partner = device(z, y_lo, core, x, 1 - y_hi)
    right = device(z, y_lo, core, (x + 1) % 4, y_hi)
    left = device(z, y_lo, core, (x + 3) % 4, y_hi)
    ways = (right, left)
    tokens, depth = n_ref.shape
    cols = out_ref.shape[1]
    half = cols // 2
    tiles = tokens // HALF

    def rows(t):
        return pl.ds(pl.multiple_of(t * HALF, HALF), HALF)

    def loads(d):
        block = 2 * ((x + REACH[d]) % 4) + y_hi
        src = w_ref.at[:, pl.ds(pl.multiple_of(block * cols, cols), cols)]
        return (
            pltpu.make_async_copy(src, wts.at[d, pl.ds(0, depth)], load_s.at[d, 0]),
            pltpu.make_async_copy(wr_ref.at[d], wts.at[d, pl.ds(depth, depth)], load_s.at[d, 1]),
        )

    own_act = pltpu.make_async_copy(n_ref, act.at[:, pl.ds(0, depth)], act_s)

    def to_partner(t):
        return remote(
            n_ref.at[rows(t)], act.at[rows(t), pl.ds(depth, depth)], y_s.at[t], y_r.at[t], partner
        )

    def pass_on(t, way):
        return remote(
            mid.at[way, rows(t)], relay.at[way, rows(t)], mid_s.at[t, way], mid_r.at[t, way],
            ways[way],
        )

    def send_direct(t, way):
        return remote(
            direct.at[way, rows(t)], final.at[way, 0, rows(t)], fin_s.at[t, way, 0],
            fin_r.at[t, way, 0], ways[way],
        )

    def send_joined(t, way):
        return remote(
            joined.at[way, rows(t)], final.at[way, 1, rows(t)], fin_s.at[t, way, 1],
            fin_r.at[t, way, 1], ways[way],
        )

    own_act.start()
    for d in range(4):
        for copy in loads(d):
            copy.start()
    greet([partner, right, left])
    for t in range(tiles):
        to_partner(t).start()
    own_act.wait()

    def product(t, d, side):
        return jnp.dot(
            act[rows(t)], wts[d, :, side * half : (side + 1) * half],
            preferred_element_type=jnp.float32,
        )

    def ready(t, d):
        @pl.when(t == 0)
        def _():
            for copy in loads(d):
                copy.wait()

    def finish(t):
        for way in range(2):
            send_direct(t, way).wait_recv()
            send_joined(t, way).wait_recv()
        r = rows(t)
        for side in range(2):
            total = own[r, side * half : (side + 1) * half]
            total = total + final[0, 1 - side, r].astype(jnp.float32)
            total = total + final[1, side, r].astype(jnp.float32)
            out_ref[r, side * half : (side + 1) * half] = total.astype(out_ref.dtype)

    def tile(t, carry):
        r = rows(t)
        to_partner(t).wait_recv()
        ready(t, 0)
        for way in range(2):
            mid[way, r] = product(t, 0, way).astype(mid.dtype)
            pass_on(t, way).start()
        for way in range(2):
            ready(t, 1 + way)
            direct[way, r] = product(t, 1 + way, 1 - way).astype(direct.dtype)
            send_direct(t, way).start()
            keep[way, r] = product(t, 1 + way, way)
        ready(t, 3)
        for side in range(2):
            own[r, side * half : (side + 1) * half] = product(t, 3, side)
        for way in range(2):
            pass_on(t, way).wait_recv()
            joined[way, r] = (keep[way, r] + relay[way, r].astype(jnp.float32)).astype(joined.dtype)
            send_joined(t, way).start()

        @pl.when(t > 0)
        def _():
            finish(t - 1)

        return carry

    lax.fori_loop(0, tiles, tile, 0)
    finish(tiles - 1)

    def drain(t, carry):
        to_partner(t).wait_send()
        for way in range(2):
            pass_on(t, way).wait_send()
            send_direct(t, way).wait_send()
            send_joined(t, way).wait_send()
        return carry

    lax.fori_loop(0, tiles, drain, 0)


def project(normed, out_weight, received):
    tokens, depth = normed.shape
    cols = out_weight.shape[1] // 8
    half = cols // 2
    tiles = tokens // HALF
    dma = pltpu.SemaphoreType.DMA
    low, wide = jnp.bfloat16, jnp.float32
    return pl.pallas_call(
        project_kernel,
        out_shape=jax.ShapeDtypeStruct((tokens, cols), low),
        in_specs=[
            pl.BlockSpec(memory_space=pltpu.VMEM),
            pl.BlockSpec(memory_space=pl.ANY),
            pl.BlockSpec(memory_space=pl.ANY),
        ],
        out_specs=pl.BlockSpec(memory_space=pltpu.VMEM),
        scratch_shapes=[
            pltpu.VMEM((tokens, 2 * depth), low),
            pltpu.VMEM((4, 2 * depth, cols), low),
            pltpu.VMEM((2, tokens, half), low),
            pltpu.VMEM((2, tokens, half), wide),
            pltpu.VMEM((2, tokens, half), low),
            pltpu.VMEM((2, tokens, half), low),
            pltpu.VMEM((tokens, cols), wide),
            pltpu.VMEM((2, tokens, half), low),
            pltpu.VMEM((2, 2, tokens, half), low),
            dma((4, 2)), dma, dma((tiles,)), dma((tiles,)), dma((tiles, 2)), dma((tiles, 2)),
            dma((tiles, 2, 2)), dma((tiles, 2, 2)),
        ],
        compiler_params=pltpu.CompilerParams(
            collective_id=2, has_side_effects=True, vmem_limit_bytes=56 << 20
        ),
        name="projection",
    )(normed, out_weight, received)


def mixer(
    x_part, z_part, bc_part, conv_x, conv_bc, dt_part, a_log, skip_scale, norm_gain, out_weight
):
    seq_count, tok_count, cols = x_part.shape
    heads = a_log.shape[0]
    blocks = 2 * seq_count
    by_block = (
        dt_part.reshape(seq_count, heads, 2, HALF).transpose(0, 2, 1, 3).reshape(blocks, heads, HALF)
    )
    normed, received = mix(
        x_part.reshape(seq_count, 2, HALF, cols),
        bc_part.reshape(seq_count, 2, HALF, 2 * STATE),
        by_block,
        a_log.reshape(heads, 1),
        jnp.repeat(skip_scale, HEAD_DIM).reshape(1, cols),
        norm_gain.reshape(1, cols),
        conv_x,
        conv_bc.reshape(KW, 2 * STATE),
        z_part.reshape(blocks, HALF, cols),
        out_weight,
    )
    projected = project(normed.reshape(seq_count * tok_count, cols), out_weight, received)
    return projected.reshape(seq_count, tok_count, projected.shape[1])


def body(x_in, z_in, bc_in, conv_x, conv_bc, dt_raw, a_log, skip_scale, norm_gain, out_weight):
    return mixer(
        x_in, z_in, bc_in, conv_x, conv_bc, dt_raw, a_log, skip_scale, norm_gain, out_weight
    )


def solution(mesh):
    in_specs = (
        P(None, "ctx", "head"),
        P(None, "ctx", "head"),
        P(None, "ctx", None, "head"),
        P(None, "head"),
        P(None, None, "head"),
        P(None, "head", "ctx"),
        P("head"),
        P("head"),
        P("head"),
        P("head", None),
    )
    out_specs = P(None, "ctx", "head")
    return jax.shard_map(body, mesh=mesh, in_specs=in_specs, out_specs=out_specs, check_vma=False)
```

time: 225 us -> 160 us (0.71)
  Pallas kernels: 125 us -> 149 us
  starting transfers between devices: 23.3 us -> 0 us
  other arithmetic: 23.9 us -> 0.63 us
  waiting for transfers between devices: 19 us -> 0 us
  local copies, waits for them, and re-layouts: 22.4 us -> 9.57 us
  matrix products: 9.22 us -> 0 us
    pallas_call x1, Pallas kernels: 55.8 us -> 79.4 us  [mix(): pl.pallas_call(mixer_kernel, out_shape=(jax.ShapeDtypeStruct((blocks, HAL...]
    all_to_all x3 -> x0, starting transfers between devices: 19.4 us -> none  [the longest x2 15.1 us: spread(): return lax.all_to_all(jnp.moveaxis(split, 2, 0), 'ctx', 0, 0)]
    all_to_all x3 -> x0, waiting for transfers between devices: 15 us -> none  [the longest x2 15 us: spread(): return lax.all_to_all(jnp.moveaxis(split, 2, 0), 'ctx', 0, 0)]
    dot_general x4 -> x0, matrix products: 9.22 us -> none  [the longest x1 5.93 us: mixer(): jnp.einsum('bhqu,buhp->bqhp', weights, xs_all, preferred_element_type=jnp...]
    unnamed x14 -> x0, other arithmetic: 8.87 us -> none
    reshape x3 -> x2, local copies, waits for them, and re-layouts: 11.5 us -> 3.32 us  [the longest x1 1.99 us: mixer(): bc_part.reshape(seq_count, 2, HALF, 2 * STATE)]
    convert_element_type x18 -> x0, other arithmetic: 5.07 us -> none  [the longest x1 2.43 us: mixer(): conv_out = sigmoid_gate(summed).astype(jnp.bfloat16)]
    ppermute x2 -> x0, waiting for transfers between devices: 4.03 us -> none  [shifted(): return lax.ppermute(block, axis, route)]
  transfers between devices with their start and end apart: 5 -> 0, of which waited for: 3 -> 0; matrix products, arithmetic and copies ran while one was open for 6% -> 0% of each run, Pallas kernels for 25% -> 0%
where the time goes in v3:
time: 160 us; the launch traced here: 159 us
  Pallas kernels  149 us (93%)
  local copies, waits for them, and re-layouts  9.57 us (6%)
    pallas_call x1, Pallas kernels, mix(): pl.pallas_call(mixer_kernel, out_shape=(jax.ShapeDtypeStruct((blocks, HAL...  79.4 us
    pallas_call x1, Pallas kernels, project(): pl.pallas_call(project_kernel, out_shape=jax.ShapeDtypeStruct((tokens, co...  69.2 us
    unnamed x2, local copies, waits for them, and re-layouts  3.95 us

profile of v3, /device:TPU:1, one launch (start us, length us, event | category | flops | bytes accessed | tf_op | source)
XLA Modules:
  0.0 158.8 jit_solution(2083512723243736669)
XLA Ops:
  0.0 1.3 copy.14
  1.3 1.3 copy.11.a_ref
  2.6 0.7 broadcast_in_dim.3
  3.3 0.7 reshape_reshape.3.skip_ref
  4.0 0.9 fusion
  4.9 0.6 pad_maximum_fusion
  5.5 2.0 %reshape.29.bc_ref = bf16[2,2,192,256]{3,2,1,0:T(8,128)(2,1)} reshape(bf16[2,384,2,128]{3,2,1,0:T(2,128)(2,1)} %param.12) | data formatting | bytes 786432 | tf_op jit(solution)/shard_map/reshape | solution.py:632
  7.5 79.4 %mixer.1 = (bf16[4,192,1024]{2,1,0:T(8,128)(2,1)}, bf16[4,1024,1024]{2,1,0:T(8,128)(2,1)}) custom-call(bf16[2,2,192,1024]{3,2,1,0:T(8,128)(2,1)} %bitcast.13, bf16[2,2,192,256]{3,2,1,0:T(8,128)(2,1)} %reshape.29.bc_ref, f32[4,16,192]{2,1,0:T(8,128)} %bitcast.15, f32[16,1]{1,0:T(8,128)} %copy.11.a_ref, f32[1,1024]{1,0:T(1,128)} %reshape_reshape.3.skip_ref, ...), custom_call_target="tpu_custom_call" | custom-call | tf_op jit(solution)/shard_map/mixer/pallas_call | solution.py:419
  86.9 69.2 %projection.1 = bf16[768,1024]{1,0:T(8,128)(2,1)} custom-call(bf16[768,1024]{1,0:T(8,128)(2,1)} %bitcast.12, bf16[1024,8192]{1,0:T(8,128)(2,1)} %w_ref.3, bf16[4,1024,1024]{2,1,0:T(8,128)(2,1)} %get-tuple-element.8.wr_ref), custom_call_target="tpu_custom_call" | custom-call | tf_op jit(solution)/shard_map/projection/pallas_call | solution.py:592
  156.1 2.7 %copy.16 = bf16[2,384,1024]{2,1,0:T(8,128)(2,1)} copy(bf16[2,384,1024]{2,1,0:T(8,128)(2,1)} %bitcast.11) | data formatting | bytes 3145728

commit v4 on v3

v4 whole, which is shorter than its diff:
```python
import jax
import jax.numpy as jnp
from jax import lax
from jax.experimental import pallas as pl
from jax.experimental.pallas import tpu as pltpu
from jax.sharding import PartitionSpec as P

HEAD_DIM = 64
STATE = 128
KW = 4
HALF = 192
MESH = pl.DeviceIdType.MESH
REACH = (2, 1, 3, 0)


def place():
    c, h = lax.axis_index("ctx"), lax.axis_index("head")
    return c // 4, (c // 2) % 2, c % 2, h // 2, h % 2


def device(z, y_lo, core, x, y_hi):
    return (z * 4 + y_lo * 2 + core, x * 2 + y_hi)


def remote(src, dst, send_sem, recv_sem, target):
    return pltpu.make_async_remote_copy(
        src_ref=src,
        dst_ref=dst,
        send_sem=send_sem,
        recv_sem=recv_sem,
        device_id=target,
        device_id_type=MESH,
    )


def rounded_parts(values):
    high = values.astype(jnp.bfloat16)
    rest = values - high.astype(jnp.float32)
    middle = rest.astype(jnp.bfloat16)
    low = (rest - middle.astype(jnp.float32)).astype(jnp.bfloat16)
    return jnp.concatenate([high, middle, low], axis=0)


def unit(size):
    rows = lax.broadcasted_iota(jnp.int32, (size, size), 0)
    cols = lax.broadcasted_iota(jnp.int32, (size, size), 1)
    return jnp.where(rows == cols, 1.0, 0.0).astype(jnp.bfloat16)


def by_rows(left, right):
    return lax.dot_general(
        left, right, (((1,), (1,)), ((), ())), preferred_element_type=jnp.float32
    )


def mixer_kernel(
    x_ref, bc_ref, dt_ref, a_ref, skip_ref, gain_ref, taps_ref, taps_bc_ref, z_ref, w_ref,
    out_ref,
    halo_x, halo_bc, wide, xs, bs, cs, cum_row, dt_row, cum_col, tail3, cum3, spread3, skips,
    scaled, upd, sib, comp, got, back, came, give, ent, dec, dec_sib, dec_chip, decs, steps, pace,
    inner, zbuf, act, wts, mid, keep, direct, joined, own, relay, final,
    z_sem, load_s, halo_s, halo_r, dec_s, dec_r, own_s, sib_s, sib_r, upd_s, upd_r, ent_s, ent_r,
    give_s, give_r, in_s, in_r, z_s, z_r, far_s, far_r, core_s, core_r,
    y_s, y_r, mid_s, mid_r, fin_s, fin_r,
):
    f32, bf16 = jnp.float32, jnp.bfloat16
    z, y_lo, core, x, y_hi = place()
    me = lax.axis_index("ctx")
    chip = me // 2
    head = lax.axis_index("head")
    cols = x_ref.shape[3]
    state_rows, lanes = got.shape[2:]
    heads = dt_ref.shape[1]
    depth = wts.shape[1] // 2
    part = depth // 8
    side_cols = cols // 2
    tiles = 4

    partner = device(z, 1 - y_lo, core, x, 1 - y_hi)
    across_y = device(z, y_lo, core, x, 1 - y_hi)
    up = device((z + 1) % 4, y_lo, core, x, y_hi)
    down = device((z + 3) % 4, y_lo, core, x, y_hi)
    other = device(z, y_lo, 1 - core, x, y_hi)
    ways = (
        device(z, y_lo, core, (x + 1) % 4, y_hi),
        device(z, y_lo, core, (x + 3) % 4, y_hi),
    )

    def at(index):
        return (index, head)

    before, after = at((me + 15) % 16), at((me + 1) % 16)

    def fellow(step):
        return (chip + step) % 8

    def of_chip(number):
        return at(2 * number + core)

    def each_fellow(work):
        def step(i, carry):
            work(i)
            return carry

        lax.fori_loop(1, 8, step, 0)

    def load(d):
        block = 2 * ((x + REACH[d]) % 4) + y_hi
        src = w_ref.at[:, pl.ds(pl.multiple_of(block * cols, cols), cols)]
        return pltpu.make_async_copy(src, wts.at[d, pl.ds(0, depth)], load_s.at[d])

    def part_at(step):
        return (((z + step) % 4) * 2 + core) * part

    def held(step):
        return pl.ds(pl.multiple_of(depth + part_at(step), part), part)

    def import_part(d):
        block = 2 * ((x + REACH[d]) % 4) + 1 - y_hi
        src = w_ref.at[
            pl.ds(pl.multiple_of(part_at(0), part), part),
            pl.ds(pl.multiple_of(block * cols, cols), cols),
        ]
        return remote(src, wts.at[d, held(0)], in_s.at[d], in_r.at[d], partner)

    def near(d, way):
        here = wts.at[d, held(0)]
        return remote(here, here, z_s.at[d, way], z_r.at[d, way], down if way else up)

    def far(d, way):
        step = 1 if way else 3
        rows = pl.ds(
            pl.multiple_of(depth + part_at(step) + way * (part // 2), part // 2), part // 2
        )
        here = wts.at[d, rows]
        return remote(here, here, far_s.at[d, way], far_r.at[d, way], down if way else up)

    def across(d, step):
        here = wts.at[d, held(step)]
        return remote(here, here, core_s.at[d, step], core_r.at[d, step], other)

    def weights_first(d):
        import_part(d).wait_recv()
        near(d, 0).start()
        near(d, 1).start()
        across(d, 0).start()

    def weights_second(d):
        for way in range(2):
            near(d, way).wait_recv()
            far(d, way).start()
            across(d, 1 if way else 3).start()

    def weights_third(d):
        far(d, 0).wait_recv()
        far(d, 1).wait_recv()
        across(d, 2).start()

    def weights_ready(d):
        load(d).wait()
        for step in range(4):
            across(d, step).wait_recv()

    def halo(half):
        target = before if half else after
        rows = pl.ds(HALF - 16, 16)
        return (
            remote(
                x_ref.at[:, half, rows], halo_x.at[half], halo_s.at[half, 0], halo_r.at[half, 0],
                target,
            ),
            remote(
                bc_ref.at[:, half, rows], halo_bc.at[half], halo_s.at[half, 1],
                halo_r.at[half, 1], target,
            ),
        )

    def share(number):
        return pl.ds(pl.multiple_of(number * state_rows, state_rows), state_rows)

    def my_lanes(which):
        return pl.ds(pl.multiple_of(which * lanes, lanes), lanes)

    def of_seq(s):
        return pl.ds(2 * s, 2)

    def swap_decay():
        return remote(dec, dec_sib, dec_s.at[0], dec_r.at[0], other)

    def send_decay(step):
        return remote(
            dec_chip, decs.at[chip], dec_s.at[step], dec_r.at[step], of_chip(fellow(step))
        )

    def swap_update(s):
        return remote(
            upd.at[of_seq(s), :, my_lanes(1 - core)], sib.at[of_seq(s)], sib_s.at[s], sib_r.at[s],
            other,
        )

    def send_update(s, step):
        owner = fellow(step)
        return remote(
            comp.at[of_seq(s), share(owner)], got.at[chip, of_seq(s)], upd_s.at[s, step],
            upd_r.at[s, step], of_chip(owner),
        )

    def send_entry(s, step):
        target = fellow(step)
        return remote(
            back.at[target, of_seq(s)], came.at[of_seq(s), share(chip)], ent_s.at[s, step],
            ent_r.at[s, step], of_chip(target),
        )

    def give_entry(s):
        return remote(
            give.at[of_seq(s)], ent.at[of_seq(s), :, my_lanes(core)], give_s.at[s], give_r.at[s],
            other,
        )

    def keep_update(s):
        return pltpu.make_async_copy(
            comp.at[of_seq(s), share(chip)], got.at[chip, of_seq(s)], own_s.at[s, 0]
        )

    def keep_entry(s):
        return pltpu.make_async_copy(
            back.at[chip, of_seq(s)], came.at[of_seq(s), share(chip)], own_s.at[s, 1]
        )

    z_copy = pltpu.make_async_copy(z_ref, zbuf, z_sem)
    z_copy.start()
    barrier = pltpu.get_barrier_semaphore()

    def hello(target):
        pl.semaphore_signal(barrier, inc=1, device_id=target, device_id_type=MESH)

    each_fellow(lambda i: hello(of_chip(fellow(i))))
    hello(at((me + 15 + 2 * core) % 16))
    for target in (other, partner, across_y) + ways:
        hello(target)

    row_id = lax.broadcasted_iota(jnp.int32, (HALF, HALF), 0)
    col_id = lax.broadcasted_iota(jnp.int32, (HALF, HALF), 1)
    causal = row_id >= col_id
    eye = unit(HALF)

    def three(values, count):
        return values[:count] + values[count : 2 * count] + values[2 * count :]

    def three_cols(values, count):
        return values[:, :count] + values[:, count : 2 * count] + values[:, 2 * count :]

    rate = -jnp.exp(three_cols(by_rows(unit(heads), rounded_parts(a_ref[...])), 1))
    dec[...] = jnp.zeros_like(dec)
    source = lax.broadcasted_iota(jnp.int32, (2 * HALF, HALF), 0)
    goal = lax.broadcasted_iota(jnp.int32, (2 * HALF, HALF), 1)
    for s in range(2):
        raw = dt_ref[s]
        both = jnp.maximum(raw, 0.0) + jnp.log1p(jnp.exp(-jnp.abs(raw)))
        sizes = rounded_parts(both)
        falls = rounded_parts(both * rate)
        for half in range(2):
            b = 2 * s + half
            low = HALF * half
            pick = jnp.where(source == goal + low, 1.0, 0.0).astype(bf16)
            ahead = jnp.where((source >= low) & (source <= goal + low), 1.0, 0.0).astype(bf16)
            step_size = three(jnp.dot(sizes, pick, preferred_element_type=f32), heads)
            cum = three(jnp.dot(falls, ahead, preferred_element_type=f32), heads)
            dt_row[b] = step_size
            cum_row[b] = cum
            col = three_cols(by_rows(eye, rounded_parts(cum)), heads)
            cum_col[b] = col
            dec[b : b + 1, :heads] = jnp.exp(col[HALF - 1 :])
            tail = jnp.exp(cum[:, HALF - 1 :] - cum) * step_size
            tail3[b] = by_rows(eye, rounded_parts(tail)).astype(bf16)
            cum3[b] = by_rows(eye, rounded_parts(jnp.exp(cum))).astype(bf16)
    of_head = lax.broadcasted_iota(jnp.int32, spread3.shape, 1) // HEAD_DIM
    of_part = lax.broadcasted_iota(jnp.int32, spread3.shape, 0) % heads
    spread3[...] = jnp.where(of_head == of_part, 1.0, 0.0).astype(bf16)
    skips[...] = three(
        jnp.dot(rounded_parts(skip_ref[...]), spread3[:heads], preferred_element_type=f32), 1
    )

    pl.semaphore_wait(barrier, 13)
    for half in range(2):
        for copy in halo(half):
            copy.start()
    swap_decay().start()
    for d in range(4):
        import_part(d).start()
    for d in range(4):
        load(d).start()

    head_id = lax.broadcasted_iota(jnp.int32, (128, lanes), 0)
    lane_head = lax.broadcasted_iota(jnp.int32, (128, lanes), 1) // HEAD_DIM
    picks = jnp.where(head_id == lane_head + core * (lanes // HEAD_DIM), 1.0, 0.0).astype(bf16)

    def to_lanes(values):
        count = values.shape[0]
        return three(jnp.dot(rounded_parts(values), picks, preferred_element_type=f32), count)

    swap_decay().wait_recv()
    dec_chip[...] = dec[...] * dec_sib[...]
    each_fellow(lambda i: send_decay(i).start())
    decs[chip] = dec_chip[...]
    pace[0] = to_lanes(dec[...])
    pace[1] = to_lanes(dec_sib[...])
    for half in range(2):
        for copy in halo(half):
            copy.wait_recv()

    turn = unit(STATE)
    chunk = 256
    band = 64

    def convolve(s, half, start, width, src, lead_ref, tap, put):
        earlier = lead_ref[0, s, :, pl.ds(start, width)]
        earlier = jnp.where(me == 0, jnp.zeros_like(earlier), earlier)
        turned = jnp.where(
            me == 15, src[s, 0, HALF - 16 :, pl.ds(start, width)],
            lead_ref[1, s, :, pl.ds(start, width)],
        )
        lead = jnp.where(half == 0, earlier, turned)
        wide[0:8] = lead.astype(f32)[8:]
        wide[8:] = src[s, half, :, pl.ds(start, width)].astype(f32)
        for r in range(0, HALF, band):
            total = tap[0:1] * wide[r + 5 : r + 5 + band]
            for k in range(1, KW):
                total = total + tap[k : k + 1] * wide[r + 5 + k : r + 5 + k + band]
            put(r, (total / (1.0 + jnp.exp(-total))).astype(bf16))

    def front(b, carry):
        s, half = b // 2, b % 2

        def put_bc(r, values):
            bs[b, r : r + band] = values[:, :STATE]
            cs[b, r : r + band] = values[:, STATE:]

        taps_bc = jnp.concatenate([taps_bc_ref[:, 0], taps_bc_ref[:, 1]], axis=1)
        convolve(s, half, 0, chunk, bc_ref, halo_bc, taps_bc, put_bc)
        bs_turned = by_rows(turn, bs[b]).astype(bf16)

        def columns(i, carry):
            start = pl.multiple_of(i * chunk, chunk)

            def put(r, values):
                xs[b, r : r + band, pl.ds(start, chunk)] = values

            convolve(s, half, start, chunk, x_ref, halo_x, taps_ref[:, pl.ds(start, chunk)], put)
            for r in range(0, HALF, band):
                factor = jnp.dot(
                    tail3[b, r : r + band], spread3[:, pl.ds(start, chunk)],
                    preferred_element_type=f32,
                )
                scaled[r : r + band] = (
                    factor * xs[b, r : r + band, pl.ds(start, chunk)].astype(f32)
                ).astype(bf16)
            upd[b, :, pl.ds(start, chunk)] = jnp.dot(
                bs_turned, scaled[...], preferred_element_type=f32
            ).astype(bf16)
            return carry

        lax.fori_loop(0, cols // chunk, columns, 0)
        return carry

    def join(s):
        swap_update(s).wait_recv()
        for half in range(2):
            b = 2 * s + half
            mine = upd[b, :, my_lanes(core)].astype(f32)
            theirs = sib[b].astype(f32)
            am_first = core == half
            later = jnp.where(am_first, pace[1, b : b + 1], pace[0, b : b + 1])
            comp[b] = (
                later * jnp.where(am_first, mine, theirs) + jnp.where(am_first, theirs, mine)
            ).astype(bf16)
        each_fellow(lambda i: send_update(s, i).start())
        keep_update(s).start()

    first = 128

    def intra(b, carry):
        scores = jnp.where(causal, by_rows(cs[b], bs[b]), 0.0)
        low_half = lax.broadcasted_iota(jnp.int32, (1, 128), 1) < HEAD_DIM
        for p in range(heads // 2):
            tops, ends = [], []
            for h in (2 * p, 2 * p + 1):
                col = cum_col[b, :, h : h + 1]
                row = cum_row[b, h : h + 1]
                size = dt_row[b, h : h + 1]
                gap = jnp.minimum(col[:first] - row[:, :first], 0.0)
                tops.append(
                    (scores[:first, :first] * jnp.exp(gap) * size[:, :first]).astype(bf16)
                )
                gap = jnp.minimum(col[first:] - row, 0.0)
                ends.append((scores[first:] * jnp.exp(gap) * size).astype(bf16))
            pair = slice(128 * p, 128 * p + 128)
            top = jnp.dot(
                jnp.concatenate(tops, axis=0), xs[b, :first, pair], preferred_element_type=f32
            )
            end = jnp.dot(
                jnp.concatenate(ends, axis=0), xs[b, :, pair], preferred_element_type=f32
            )
            inner[b, :first, pair] = jnp.where(low_half, top[:first], top[first:])
            rest = HALF - first
            inner[b, first:, pair] = jnp.where(low_half, end[:rest], end[rest:])
        return carry

    def chain(s):
        each_fellow(lambda i: send_update(s, i).wait_recv())
        keep_update(s).wait()
        state = jnp.zeros((state_rows, lanes), f32)
        for i in range(16):
            c, half = (i, 0) if i < 8 else (15 - i, 1)
            b = 2 * s + half
            back[c, b] = state.astype(bf16)
            state = steps[8 * c + b : 8 * c + b + 1] * state + got[c, b].astype(f32)
        each_fellow(lambda i: send_entry(s, i).start())
        keep_entry(s).start()

    def enter(s):
        each_fellow(lambda i: send_entry(s, i).wait_recv())
        keep_entry(s).wait()
        for half in range(2):
            b = 2 * s + half
            mine = upd[b, :, my_lanes(core)].astype(f32)
            theirs = sib[b].astype(f32)
            am_first = core == half
            entry = came[b].astype(f32)
            rate_first = jnp.where(am_first, pace[0, b : b + 1], pace[1, b : b + 1])
            second = rate_first * entry + jnp.where(am_first, mine, theirs)
            ent[b, :, my_lanes(core)] = jnp.where(am_first, entry, second).astype(bf16)
            give[b] = jnp.where(am_first, second, entry).astype(bf16)
        give_entry(s).start()

    def tile_rows(t):
        return pl.ds(pl.multiple_of(t * HALF, HALF), HALF)

    def to_partner(t):
        return remote(
            act.at[tile_rows(t), pl.ds(0, depth)], act.at[tile_rows(t), pl.ds(depth, depth)],
            y_s.at[t], y_r.at[t], across_y,
        )

    def finish(b, carry):
        squares = [jnp.zeros((96, 128), f32)] * 2
        for q in range(cols // chunk):
            part_cols = slice(q * chunk, (q + 1) * chunk)
            for i in range(2):
                r = slice(96 * i, 96 * i + 96)
                carried = jnp.dot(cs[b, r], ent[b, :, part_cols], preferred_element_type=f32)
                factor = jnp.dot(cum3[b, r], spread3[:, part_cols], preferred_element_type=f32)
                total = inner[b, r, part_cols] + factor * carried
                total = total + skips[:, part_cols] * xs[b, r, part_cols].astype(f32)
                gate = zbuf[b, r, part_cols].astype(f32)
                total = total * (gate / (1.0 + jnp.exp(-gate)))
                inner[b, r, part_cols] = total
                square = total * total
                squares[i] = squares[i] + square[:, :128] + square[:, 128:]
        for i in range(2):
            spread = jnp.sum(squares[i], axis=1, keepdims=True) * (1.0 / cols)
            scale = lax.rsqrt(spread + 1e-05)
            r = slice(96 * i, 96 * i + 96)
            to = pl.ds(pl.multiple_of(b * HALF + 96 * i, 96), 96)
            for q in range(cols // chunk):
                part_cols = slice(q * chunk, (q + 1) * chunk)
                act[to, part_cols] = (
                    inner[b, r, part_cols] * scale * gain_ref[:, part_cols]
                ).astype(bf16)
        to_partner(b).start()
        return carry

    def pass_on(t, way):
        return remote(
            mid.at[way, tile_rows(t)], relay.at[way, tile_rows(t)], mid_s.at[t, way],
            mid_r.at[t, way], ways[way],
        )

    def send_direct(t, way):
        return remote(
            direct.at[way, tile_rows(t)], final.at[way, 0, tile_rows(t)], fin_s.at[t, way, 0],
            fin_r.at[t, way, 0], ways[way],
        )

    def send_joined(t, way):
        return remote(
            joined.at[way, tile_rows(t)], final.at[way, 1, tile_rows(t)], fin_s.at[t, way, 1],
            fin_r.at[t, way, 1], ways[way],
        )

    def side_of(side):
        return slice(side * side_cols, (side + 1) * side_cols)

    def product(t, d, side):
        return jnp.dot(
            act[tile_rows(t)], wts[d, :, side_of(side)], preferred_element_type=f32
        )

    def project_far(t):
        to_partner(t).wait_recv()
        for way in range(2):
            mid[way, tile_rows(t)] = product(t, 0, way).astype(bf16)
            pass_on(t, way).start()

    def project_near(t, way):
        direct[way, tile_rows(t)] = product(t, 1 + way, 1 - way).astype(bf16)
        send_direct(t, way).start()
        keep[way, tile_rows(t)] = product(t, 1 + way, way)

    def project_join(t):
        for way in range(2):
            pass_on(t, way).wait_recv()
            r = tile_rows(t)
            joined[way, r] = (keep[way, r] + relay[way, r].astype(f32)).astype(bf16)
            send_joined(t, way).start()

    def project_own(t):
        for side in range(2):
            own[tile_rows(t), side_of(side)] = product(t, 3, side)

    def project_end(t):
        r = tile_rows(t)
        for way in range(2):
            send_direct(t, way).wait_recv()
            send_joined(t, way).wait_recv()
        for side in range(2):
            total = own[r, side_of(side)] + final[0, 1 - side, r].astype(f32)
            total = total + final[1, side, r].astype(f32)
            out_ref[r, side_of(side)] = total.astype(bf16)

    for s in range(2):
        lax.fori_loop(2 * s, 2 * s + 2, front, 0)
        swap_update(s).start()
    weights_first(0)
    join(0)
    join(1)
    weights_first(1)
    lax.fori_loop(0, 2, intra, 0)
    each_fellow(lambda i: send_decay(i).wait_recv())
    steps[...] = to_lanes(decs[...].reshape(64, 128))
    chain(0)
    weights_second(0)
    weights_first(2)
    lax.fori_loop(2, 4, intra, 0)
    chain(1)
    weights_second(1)
    weights_first(3)
    weights_third(0)
    z_copy.wait()
    enter(0)
    give_entry(0).wait_recv()
    lax.fori_loop(0, 2, finish, 0)
    enter(1)
    weights_second(2)
    weights_third(1)
    give_entry(1).wait_recv()
    lax.fori_loop(2, 4, finish, 0)
    weights_second(3)
    weights_third(2)
    weights_ready(0)
    project_far(0)
    weights_third(3)
    weights_ready(1)
    project_near(0, 0)
    weights_ready(2)
    project_near(0, 1)

    def middle(t, carry):
        project_far(t)
        for way in range(2):
            project_near(t, way)
        project_join(t - 1)
        return carry

    lax.fori_loop(1, tiles, middle, 0)
    project_join(tiles - 1)
    weights_ready(3)

    def last(t, carry):
        project_own(t)
        project_end(t)
        return carry

    lax.fori_loop(0, tiles, last, 0)

    for half in range(2):
        for copy in halo(half):
            copy.wait_send()
    swap_decay().wait_send()
    for s in range(2):
        swap_update(s).wait_send()
        give_entry(s).wait_send()

    def drain(i):
        send_decay(i).wait_send()
        for s in range(2):
            send_update(s, i).wait_send()
            send_entry(s, i).wait_send()

    each_fellow(drain)
    for d in range(4):
        import_part(d).wait_send()
        for way in range(2):
            near(d, way).wait_send()
            far(d, way).wait_send()
        for step in range(4):
            across(d, step).wait_send()

    def drain_tile(t, carry):
        to_partner(t).wait_send()
        for way in range(2):
            pass_on(t, way).wait_send()
            send_direct(t, way).wait_send()
            send_joined(t, way).wait_send()
        return carry

    lax.fori_loop(0, tiles, drain_tile, 0)


def mix(x_part, bc_part, dt_part, a_log, skip_scale, norm_gain, conv_x, conv_bc, z_part, weight):
    blocks = 4
    heads = dt_part.shape[1]
    cols = x_part.shape[3]
    depth = weight.shape[0]
    tokens = blocks * HALF
    half = cols // 2
    dma = pltpu.SemaphoreType.DMA
    low, wide = jnp.bfloat16, jnp.float32
    vmem = pl.BlockSpec(memory_space=pltpu.VMEM)
    hbm = pl.BlockSpec(memory_space=pl.ANY)
    return pl.pallas_call(
        mixer_kernel,
        out_shape=jax.ShapeDtypeStruct((tokens, cols), low),
        in_specs=[vmem] * 8 + [hbm] * 2,
        out_specs=vmem,
        scratch_shapes=[
            pltpu.VMEM((2, 2, 16, cols), low),
            pltpu.VMEM((2, 2, 16, 2 * STATE), low),
            pltpu.VMEM((8 + HALF, 256), wide),
            pltpu.VMEM((blocks, HALF, cols), low),
            pltpu.VMEM((blocks, HALF, STATE), low),
            pltpu.VMEM((blocks, HALF, STATE), low),
            pltpu.VMEM((blocks, heads, HALF), wide),
            pltpu.VMEM((blocks, heads, HALF), wide),
            pltpu.VMEM((blocks, HALF, heads), wide),
            pltpu.VMEM((blocks, HALF, 3 * heads), low),
            pltpu.VMEM((blocks, HALF, 3 * heads), low),
            pltpu.VMEM((3 * heads, cols), low),
            pltpu.VMEM((1, cols), wide),
            pltpu.VMEM((HALF, 256), low),
            pltpu.VMEM((blocks, STATE, cols), low),
            pltpu.VMEM((blocks, STATE, half), low),
            pltpu.VMEM((blocks, STATE, half), low),
            pltpu.VMEM((8, blocks, STATE // 8, half), low),
            pltpu.VMEM((8, blocks, STATE // 8, half), low),
            pltpu.VMEM((blocks, STATE, half), low),
            pltpu.VMEM((blocks, STATE, half), low),
            pltpu.VMEM((blocks, STATE, cols), low),
            pltpu.VMEM((8, 128), wide),
            pltpu.VMEM((8, 128), wide),
            pltpu.VMEM((8, 128), wide),
            pltpu.VMEM((8, 8, 128), wide),
            pltpu.VMEM((64, half), wide),
            pltpu.VMEM((2, 8, half), wide),
            pltpu.VMEM((blocks, HALF, cols), wide),
            pltpu.VMEM((blocks, HALF, cols), low),
            pltpu.VMEM((tokens, 2 * depth), low),
            pltpu.VMEM((4, 2 * depth, cols), low),
            pltpu.VMEM((2, tokens, half), low),
            pltpu.VMEM((2, tokens, half), wide),
            pltpu.VMEM((2, tokens, half), low),
            pltpu.VMEM((2, tokens, half), low),
            pltpu.VMEM((tokens, cols), wide),
            pltpu.VMEM((2, tokens, half), low),
            pltpu.VMEM((2, 2, tokens, half), low),
            dma, dma((4,)), dma((2, 2)), dma((2, 2)), dma((8,)), dma((8,)), dma((2, 2)),
            dma((2,)), dma((2,)), dma((2, 8)), dma((2, 8)), dma((2, 8)), dma((2, 8)),
            dma((2,)), dma((2,)), dma((4,)), dma((4,)), dma((4, 2)), dma((4, 2)),
            dma((4, 2)), dma((4, 2)), dma((4, 4)), dma((4, 4)),
            dma((blocks,)), dma((blocks,)), dma((blocks, 2)), dma((blocks, 2)),
            dma((blocks, 2, 2)), dma((blocks, 2, 2)),
        ],
        compiler_params=pltpu.CompilerParams(
            collective_id=1, has_side_effects=True, vmem_limit_bytes=60 << 20
        ),
        name="mixer",
    )(x_part, bc_part, dt_part, a_log, skip_scale, norm_gain, conv_x, conv_bc, z_part, weight)


def mixer(
    x_part, z_part, bc_part, conv_x, conv_bc, dt_part, a_log, skip_scale, norm_gain, out_weight
):
    seq_count, tok_count, cols = x_part.shape
    heads = a_log.shape[0]
    projected = mix(
        x_part.reshape(seq_count, 2, HALF, cols),
        bc_part.reshape(seq_count, 2, HALF, 2 * STATE),
        dt_part,
        a_log.reshape(1, heads),
        skip_scale.reshape(1, heads),
        norm_gain.reshape(1, cols),
        conv_x,
        conv_bc,
        z_part.reshape(2 * seq_count, HALF, cols),
        out_weight,
    )
    return projected.reshape(seq_count, tok_count, cols)


def body(x_in, z_in, bc_in, conv_x, conv_bc, dt_raw, a_log, skip_scale, norm_gain, out_weight):
    return mixer(
        x_in, z_in, bc_in, conv_x, conv_bc, dt_raw, a_log, skip_scale, norm_gain, out_weight
    )


def solution(mesh):
    in_specs = (
        P(None, "ctx", "head"),
        P(None, "ctx", "head"),
        P(None, "ctx", None, "head"),
        P(None, "head"),
        P(None, None, "head"),
        P(None, "head", "ctx"),
        P("head"),
        P("head"),
        P("head"),
        P("head", None),
    )
    out_specs = P(None, "ctx", "head")
    return jax.shard_map(body, mesh=mesh, in_specs=in_specs, out_specs=out_specs, check_vma=False)
```

time: 160 us -> 126 us (0.79)
  Pallas kernels: 149 us -> 121 us
  local copies, waits for them, and re-layouts: 9.57 us -> 4.66 us
    pallas_call x2 -> x1, Pallas kernels: 149 us -> 121 us  [mix(): pl.pallas_call(mixer_kernel, out_shape=jax.ShapeDtypeStruct((tokens, cols...]
    unnamed x2 -> x1, local copies, waits for them, and re-layouts: 3.95 us -> 2.67 us
where the time goes in v4:
time: 126 us
  Pallas kernels  121 us (96%)
  local copies, waits for them, and re-layouts  4.66 us (4%)
    pallas_call x1, Pallas kernels, mix(): pl.pallas_call(mixer_kernel, out_shape=jax.ShapeDtypeStruct((tokens, cols...  121 us
    unnamed x1, local copies, waits for them, and re-layouts  2.67 us

profile of v4, /device:TPU:1, one launch (start us, length us, event | category | flops | bytes accessed | tf_op | source)
XLA Modules:
  0.0 126.0 jit_solution(7539236142235544228)
XLA Ops:
  0.0 2.0 %reshape.22.bc_ref = bf16[2,2,192,256]{3,2,1,0:T(8,128)(2,1)} reshape(bf16[2,384,2,128]{3,2,1,0:T(2,128)(2,1)} %param.12) | data formatting | bytes 786432 | tf_op jit(solution)/shard_map/reshape | solution.py:698
  2.0 121.3 %mixer.1 = bf16[768,1024]{1,0:T(8,128)(2,1)} custom-call(bf16[2,2,192,1024]{3,2,1,0:T(8,128)(2,1)} %bitcast.7, bf16[2,2,192,256]{3,2,1,0:T(8,128)(2,1)} %reshape.22.bc_ref, f32[2,16,384]{2,1,0:T(8,128)} %dt_ref.1, f32[1,16]{1,0:T(1,128)} %bitcast.10, f32[1,16]{1,0:T(1,128)} %bitcast.11, f32[1,1024]{1,0:T(1,128)} %bitcast.9, f32[4,1024]{1,0:T(4,128)} %taps_ref.1, ...), custom_call_target="tpu_custom_call" | custom-call | tf_op jit(solution)/shard_map/mixer/pallas_call | solution.py:632
  123.3 2.7 %copy.12 = bf16[2,384,1024]{2,1,0:T(8,128)(2,1)} copy(bf16[2,384,1024]{2,1,0:T(8,128)(2,1)} %bitcast.6) | data formatting | bytes 3145728

commit v5 on v4

--- a/solution.py
+++ b/solution.py
@@ -60,7 +60,7 @@
     scaled, upd, sib, comp, got, back, came, give, ent, dec, dec_sib, dec_chip, decs, steps, pace,
     inner, zbuf, act, wts, mid, keep, direct, joined, own, relay, final,
     z_sem, load_s, halo_s, halo_r, dec_s, dec_r, own_s, sib_s, sib_r, upd_s, upd_r, ent_s, ent_r,
-    give_s, give_r, in_s, in_r, z_s, z_r, far_s, far_r, core_s, core_r,
+    give_s, give_r, in_s, in_r, side_s, side_r, near_s, near_r, far_s, far_r, core_s, core_r,
     y_s, y_r, mid_s, mid_r, fin_s, fin_r,
 ):
     f32, bf16 = jnp.float32, jnp.bfloat16
@@ -72,7 +72,7 @@
     state_rows, lanes = got.shape[2:]
     heads = dt_ref.shape[1]
     depth = wts.shape[1] // 2
-    part = depth // 8
+    part = depth // 16
     side_cols = cols // 2
     tiles = 4
 
@@ -80,6 +80,7 @@
     across_y = device(z, y_lo, core, x, 1 - y_hi)
     up = device((z + 1) % 4, y_lo, core, x, y_hi)
     down = device((z + 3) % 4, y_lo, core, x, y_hi)
+    beside = device(z, 1 - y_lo, core, x, y_hi)
     other = device(z, y_lo, 1 - core, x, y_hi)
     ways = (
         device(z, y_lo, core, (x + 1) % 4, y_hi),
@@ -109,57 +110,68 @@
         src = w_ref.at[:, pl.ds(pl.multiple_of(block * cols, cols), cols)]
         return pltpu.make_async_copy(src, wts.at[d, pl.ds(0, depth)], load_s.at[d])
 
-    def part_at(step):
-        return (((z + step) % 4) * 2 + core) * part
-
-    def held(step):
-        return pl.ds(pl.multiple_of(depth + part_at(step), part), part)
+    def piece(step, low, base, count=1):
+        number = (((z + step) % 4) * 2 + core) * 2 + low
+        return pl.ds(pl.multiple_of(base + number * part, part), count * part)
 
     def import_part(d):
         block = 2 * ((x + REACH[d]) % 4) + 1 - y_hi
-        src = w_ref.at[
-            pl.ds(pl.multiple_of(part_at(0), part), part),
-            pl.ds(pl.multiple_of(block * cols, cols), cols),
-        ]
-        return remote(src, wts.at[d, held(0)], in_s.at[d], in_r.at[d], partner)
-
-    def near(d, way):
-        here = wts.at[d, held(0)]
-        return remote(here, here, z_s.at[d, way], z_r.at[d, way], down if way else up)
+        rows = piece(0, 1 - y_lo, 0)
+        src = w_ref.at[rows, pl.ds(pl.multiple_of(block * cols, cols), cols)]
+        there = wts.at[d, piece(0, 1 - y_lo, depth)]
+        return remote(src, there, in_s.at[d], in_r.at[d], partner)
+
+    def swap_part(d):
+        here = wts.at[d, piece(0, y_lo, depth)]
+        return remote(here, here, side_s.at[d], side_r.at[d], beside)
+
+    def near(d, way, swapped):
+        here = wts.at[d, piece(0, 1 - y_lo if swapped else y_lo, depth)]
+        return remote(
+            here, here, near_s.at[d, way, swapped], near_r.at[d, way, swapped],
+            down if way else up,
+        )
 
     def far(d, way):
-        step = 1 if way else 3
-        rows = pl.ds(
-            pl.multiple_of(depth + part_at(step) + way * (part // 2), part // 2), part // 2
-        )
+        here = wts.at[d, piece(1 if way else 3, way, depth)]
+        return remote(here, here, far_s.at[d, way], far_r.at[d, way], down if way else up)
+
+    def across(d, number):
+        if number < 2:
+            rows = piece(0, 1 - y_lo if number else y_lo, depth)
+        else:
+            rows = piece((1, 3, 2)[number - 2], 0, depth, 2)
         here = wts.at[d, rows]
-        return remote(here, here, far_s.at[d, way], far_r.at[d, way], down if way else up)
-
-    def across(d, step):
-        here = wts.at[d, held(step)]
-        return remote(here, here, core_s.at[d, step], core_r.at[d, step], other)
-
-    def weights_first(d):
+        return remote(here, here, core_s.at[d, number], core_r.at[d, number], other)
+
+    def weights_in(d):
         import_part(d).wait_recv()
-        near(d, 0).start()
-        near(d, 1).start()
+        swap_part(d).start()
         across(d, 0).start()
 
-    def weights_second(d):
+    def weights_near(d, swapped):
+        if swapped:
+            swap_part(d).wait_recv()
+            across(d, 1).start()
         for way in range(2):
-            near(d, way).wait_recv()
+            near(d, way, swapped).start()
+
+    def weights_far(d):
+        for way in range(2):
+            for swapped in range(2):
+                near(d, way, swapped).wait_recv()
             far(d, way).start()
-            across(d, 1 if way else 3).start()
-
-    def weights_third(d):
+            across(d, 2 if way else 3).start()
+
+    def weights_last(d):
         far(d, 0).wait_recv()
         far(d, 1).wait_recv()
-        across(d, 2).start()
+        across(d, 4).start()
 
     def weights_ready(d):
         load(d).wait()
-        for step in range(4):
-            across(d, step).wait_recv()
+        for number in range(5):
+            across(d, number).wait_recv()
 
     def halo(half):
         target = before if half else after
@@ -255,7 +267,7 @@
     dec[...] = jnp.zeros_like(dec)
     source = lax.broadcasted_iota(jnp.int32, (2 * HALF, HALF), 0)
     goal = lax.broadcasted_iota(jnp.int32, (2 * HALF, HALF), 1)
-    for s in range(2):
+    def decays(s):
         raw = dt_ref[s]
         both = jnp.maximum(raw, 0.0) + jnp.log1p(jnp.exp(-jnp.abs(raw)))
         sizes = rounded_parts(both)
@@ -275,6 +287,17 @@
             tail = jnp.exp(cum[:, HALF - 1 :] - cum) * step_size
             tail3[b] = by_rows(eye, rounded_parts(tail)).astype(bf16)
             cum3[b] = by_rows(eye, rounded_parts(jnp.exp(cum))).astype(bf16)
+    decays(0)
+    pl.semaphore_wait(barrier, 13)
+    for half in range(2):
+        for copy in halo(half):
+            copy.start()
+    for d in range(4):
+        import_part(d).start()
+    decays(1)
+    swap_decay().start()
+    for d in range(4):
+        load(d).start()
     of_head = lax.broadcasted_iota(jnp.int32, spread3.shape, 1) // HEAD_DIM
     of_part = lax.broadcasted_iota(jnp.int32, spread3.shape, 0) % heads
     spread3[...] = jnp.where(of_head == of_part, 1.0, 0.0).astype(bf16)
@@ -282,16 +305,6 @@
         jnp.dot(rounded_parts(skip_ref[...]), spread3[:heads], preferred_element_type=f32), 1
     )
 
-    pl.semaphore_wait(barrier, 13)
-    for half in range(2):
-        for copy in halo(half):
-            copy.start()
-    swap_decay().start()
-    for d in range(4):
-        import_part(d).start()
-    for d in range(4):
-        load(d).start()
-
     head_id = lax.broadcasted_iota(jnp.int32, (128, lanes), 0)
     lane_head = lax.broadcasted_iota(jnp.int32, (128, lanes), 1) // HEAD_DIM
     picks = jnp.where(head_id == lane_head + core * (lanes // HEAD_DIM), 1.0, 0.0).astype(bf16)
@@ -300,15 +313,13 @@
         count = values.shape[0]
         return three(jnp.dot(rounded_parts(values), picks, preferred_element_type=f32), count)
 
-    swap_decay().wait_recv()
-    dec_chip[...] = dec[...] * dec_sib[...]
-    each_fellow(lambda i: send_decay(i).start())
-    decs[chip] = dec_chip[...]
-    pace[0] = to_lanes(dec[...])
-    pace[1] = to_lanes(dec_sib[...])
-    for half in range(2):
-        for copy in halo(half):
-            copy.wait_recv()
+    def chip_decays():
+        swap_decay().wait_recv()
+        dec_chip[...] = dec[...] * dec_sib[...]
+        each_fellow(lambda i: send_decay(i).start())
+        decs[chip] = dec_chip[...]
+        pace[0] = to_lanes(dec[...])
+        pace[1] = to_lanes(dec_sib[...])
 
     turn = unit(STATE)
     chunk = 256
@@ -529,60 +540,83 @@
             total = total + final[1, side, r].astype(f32)
             out_ref[r, side_of(side)] = total.astype(bf16)
 
-    for s in range(2):
-        lax.fori_loop(2 * s, 2 * s + 2, front, 0)
-        swap_update(s).start()
-    weights_first(0)
+    def loop(start, stop, work):
+        lax.fori_loop(start, stop, work, 0)
+
+    for half in range(2):
+        for copy in halo(half):
+            copy.wait_recv()
+    loop(0, 2, front)
+    swap_update(0).start()
+    chip_decays()
+    weights_in(0)
+    weights_near(0, 0)
+    loop(2, 3, front)
     join(0)
+    weights_in(1)
+    weights_near(0, 1)
+    loop(3, 4, front)
+    swap_update(1).start()
+    loop(0, 1, intra)
     join(1)
-    weights_first(1)
-    lax.fori_loop(0, 2, intra, 0)
+    weights_in(2)
+    weights_in(3)
+    loop(1, 2, intra)
     each_fellow(lambda i: send_decay(i).wait_recv())
     steps[...] = to_lanes(decs[...].reshape(64, 128))
     chain(0)
-    weights_second(0)
-    weights_first(2)
-    lax.fori_loop(2, 4, intra, 0)
+    weights_far(0)
+    loop(2, 3, intra)
     chain(1)
-    weights_second(1)
-    weights_first(3)
-    weights_third(0)
+    weights_near(1, 0)
+    weights_near(1, 1)
     z_copy.wait()
     enter(0)
+    weights_last(0)
+    loop(3, 4, intra)
     give_entry(0).wait_recv()
-    lax.fori_loop(0, 2, finish, 0)
+    loop(0, 2, finish)
+    weights_near(2, 0)
+    weights_near(2, 1)
     enter(1)
-    weights_second(2)
-    weights_third(1)
+    weights_far(1)
     give_entry(1).wait_recv()
-    lax.fori_loop(2, 4, finish, 0)
-    weights_second(3)
-    weights_third(2)
+    loop(2, 4, finish)
+    weights_far(2)
+    weights_last(1)
+    weights_near(3, 0)
+    weights_near(3, 1)
     weights_ready(0)
     project_far(0)
-    weights_third(3)
+    weights_last(2)
     weights_ready(1)
     project_near(0, 0)
     weights_ready(2)
     project_near(0, 1)
+    weights_far(3)
+    project_join(0)
+    project_far(1)
+    project_near(1, 0)
+    project_near(1, 1)
+    weights_last(3)
+    weights_ready(3)
 
     def middle(t, carry):
         project_far(t)
-        for way in range(2):
-            project_near(t, way)
         project_join(t - 1)
+        project_near(t, 0)
+        project_near(t, 1)
+        project_own(t - 2)
         return carry
 
-    lax.fori_loop(1, tiles, middle, 0)
+    loop(2, tiles, middle)
     project_join(tiles - 1)
-    weights_ready(3)
-
-    def last(t, carry):
+
+    def rest(t, carry):
         project_own(t)
-        project_end(t)
         return carry
 
-    lax.fori_loop(0, tiles, last, 0)
+    loop(tiles - 2, tiles, rest)
 
     for half in range(2):
         for copy in halo(half):
@@ -601,21 +635,25 @@
     each_fellow(drain)
     for d in range(4):
         import_part(d).wait_send()
+        swap_part(d).wait_send()
         for way in range(2):
-            near(d, way).wait_send()
             far(d, way).wait_send()
-        for step in range(4):
-            across(d, step).wait_send()
-
-    def drain_tile(t, carry):
+            for swapped in range(2):
+                near(d, way, swapped).wait_send()
+        for number in range(5):
+            across(d, number).wait_send()
+
+    def last(t, carry):
         to_partner(t).wait_send()
         for way in range(2):
             pass_on(t, way).wait_send()
             send_direct(t, way).wait_send()
+        project_end(t)
+        for way in range(2):
             send_joined(t, way).wait_send()
         return carry
 
-    lax.fori_loop(0, tiles, drain_tile, 0)
+    loop(0, tiles, last)
 
 
 def mix(x_part, bc_part, dt_part, a_log, skip_scale, norm_gain, conv_x, conv_bc, z_part, weight):
@@ -676,8 +714,8 @@
             pltpu.VMEM((2, 2, tokens, half), low),
             dma, dma((4,)), dma((2, 2)), dma((2, 2)), dma((8,)), dma((8,)), dma((2, 2)),
             dma((2,)), dma((2,)), dma((2, 8)), dma((2, 8)), dma((2, 8)), dma((2, 8)),
-            dma((2,)), dma((2,)), dma((4,)), dma((4,)), dma((4, 2)), dma((4, 2)),
-            dma((4, 2)), dma((4, 2)), dma((4, 4)), dma((4, 4)),
+            dma((2,)), dma((2,)), dma((4,)), dma((4,)), dma((4,)), dma((4,)),
+            dma((4, 2, 2)), dma((4, 2, 2)), dma((4, 2)), dma((4, 2)), dma((4, 5)), dma((4, 5)),
             dma((blocks,)), dma((blocks,)), dma((blocks, 2)), dma((blocks, 2)),
             dma((blocks, 2, 2)), dma((blocks, 2, 2)),
         ],

time: 126 us -> 115 us (0.913)
  Pallas kernels: 121 us -> 110 us
    pallas_call x1, Pallas kernels: 121 us -> 110 us  [mix(): pl.pallas_call(mixer_kernel, out_shape=jax.ShapeDtypeStruct((tokens, cols...]
where the time goes in v5:
time: 115 us; the launch traced here: 114 us
  Pallas kernels  110 us (96%)
  local copies, waits for them, and re-layouts  4.66 us (4%)
    pallas_call x1, Pallas kernels, mix(): pl.pallas_call(mixer_kernel, out_shape=jax.ShapeDtypeStruct((tokens, cols...  110 us
    unnamed x1, local copies, waits for them, and re-layouts  2.67 us

profile of v5, /device:TPU:1, one launch (start us, length us, event | category | flops | bytes accessed | tf_op | source)
XLA Modules:
  0.0 114.3 jit_solution(16664021300133184433)
XLA Ops:
  0.0 2.0 %reshape.22.bc_ref = bf16[2,2,192,256]{3,2,1,0:T(8,128)(2,1)} reshape(bf16[2,384,2,128]{3,2,1,0:T(2,128)(2,1)} %param.12) | data formatting | bytes 786432 | tf_op jit(solution)/shard_map/reshape | solution.py:736
  2.0 109.6 %mixer.1 = bf16[768,1024]{1,0:T(8,128)(2,1)} custom-call(bf16[2,2,192,1024]{3,2,1,0:T(8,128)(2,1)} %bitcast.7, bf16[2,2,192,256]{3,2,1,0:T(8,128)(2,1)} %reshape.22.bc_ref, f32[2,16,384]{2,1,0:T(8,128)} %dt_ref.1, f32[1,16]{1,0:T(1,128)} %bitcast.10, f32[1,16]{1,0:T(1,128)} %bitcast.11, f32[1,1024]{1,0:T(1,128)} %bitcast.9, f32[4,1024]{1,0:T(4,128)} %taps_ref.1, ...), custom_call_target="tpu_custom_call" | custom-call | tf_op jit(solution)/shard_map/mixer/pallas_call | solution.py:670
  111.6 2.7 %copy.12 = bf16[2,384,1024]{2,1,0:T(8,128)(2,1)} copy(bf16[2,384,1024]{2,1,0:T(8,128)(2,1)} %bitcast.6) | data formatting | bytes 3145728

commit v6 on v5

--- a/solution.py
+++ b/solution.py
@@ -325,16 +325,7 @@
     chunk = 256
     band = 64
 
-    def convolve(s, half, start, width, src, lead_ref, tap, put):
-        earlier = lead_ref[0, s, :, pl.ds(start, width)]
-        earlier = jnp.where(me == 0, jnp.zeros_like(earlier), earlier)
-        turned = jnp.where(
-            me == 15, src[s, 0, HALF - 16 :, pl.ds(start, width)],
-            lead_ref[1, s, :, pl.ds(start, width)],
-        )
-        lead = jnp.where(half == 0, earlier, turned)
-        wide[0:8] = lead.astype(f32)[8:]
-        wide[8:] = src[s, half, :, pl.ds(start, width)].astype(f32)
+    def convolve(tap, put):
         for r in range(0, HALF, band):
             total = tap[0:1] * wide[r + 5 : r + 5 + band]
             for k in range(1, KW):
@@ -344,12 +335,23 @@
     def front(b, carry):
         s, half = b // 2, b % 2
 
+        taps_bc = jnp.concatenate([taps_bc_ref[:, 0], taps_bc_ref[:, 1]], axis=1)
+
         def put_bc(r, values):
             bs[b, r : r + band] = values[:, :STATE]
             cs[b, r : r + band] = values[:, STATE:]
 
-        taps_bc = jnp.concatenate([taps_bc_ref[:, 0], taps_bc_ref[:, 1]], axis=1)
-        convolve(s, half, 0, chunk, bc_ref, halo_bc, taps_bc, put_bc)
+        def split(values):
+            return jnp.concatenate([values[:, 0], values[:, 1]], axis=1).astype(f32)
+
+        earlier = split(halo_bc[0, s])
+        earlier = jnp.where(me == 0, jnp.zeros_like(earlier), earlier)
+        turned = jnp.where(
+            me == 15, split(bc_ref[s, 0, HALF - 16 :]), split(halo_bc[1, s])
+        )
+        wide[0:8] = jnp.where(half == 0, earlier, turned)[8:]
+        wide[8:] = split(bc_ref[s, half])
+        convolve(taps_bc, put_bc)
         bs_turned = by_rows(turn, bs[b]).astype(bf16)
 
         def columns(i, carry):
@@ -358,7 +360,13 @@
             def put(r, values):
                 xs[b, r : r + band, pl.ds(start, chunk)] = values
 
-            convolve(s, half, start, chunk, x_ref, halo_x, taps_ref[:, pl.ds(start, chunk)], put)
+            here = pl.ds(start, chunk)
+            earlier = halo_x[0, s, :, here]
+            earlier = jnp.where(me == 0, jnp.zeros_like(earlier), earlier)
+            turned = jnp.where(me == 15, x_ref[s, 0, HALF - 16 :, here], halo_x[1, s, :, here])
+            wide[0:8] = jnp.where(half == 0, earlier, turned).astype(f32)[8:]
+            wide[8:] = x_ref[s, half, :, here].astype(f32)
+            convolve(taps_ref[:, here], put)
             for r in range(0, HALF, band):
                 factor = jnp.dot(
                     tail3[b, r : r + band], spread3[:, pl.ds(start, chunk)],
@@ -669,12 +677,12 @@
     hbm = pl.BlockSpec(memory_space=pl.ANY)
     return pl.pallas_call(
         mixer_kernel,
-        out_shape=jax.ShapeDtypeStruct((tokens, cols), low),
+        out_shape=pltpu.VMEM((tokens, cols), low),
         in_specs=[vmem] * 8 + [hbm] * 2,
         out_specs=vmem,
         scratch_shapes=[
             pltpu.VMEM((2, 2, 16, cols), low),
-            pltpu.VMEM((2, 2, 16, 2 * STATE), low),
+            pltpu.VMEM((2, 2, 16, 2, STATE), low),
             pltpu.VMEM((8 + HALF, 256), wide),
             pltpu.VMEM((blocks, HALF, cols), low),
             pltpu.VMEM((blocks, HALF, STATE), low),
@@ -720,7 +728,7 @@
             dma((blocks, 2, 2)), dma((blocks, 2, 2)),
         ],
         compiler_params=pltpu.CompilerParams(
-            collective_id=1, has_side_effects=True, vmem_limit_bytes=60 << 20
+            collective_id=1, has_side_effects=True, vmem_limit_bytes=58 << 20
         ),
         name="mixer",
     )(x_part, bc_part, dt_part, a_log, skip_scale, norm_gain, conv_x, conv_bc, z_part, weight)
@@ -733,7 +741,7 @@
     heads = a_log.shape[0]
     projected = mix(
         x_part.reshape(seq_count, 2, HALF, cols),
-        bc_part.reshape(seq_count, 2, HALF, 2 * STATE),
+        bc_part.reshape(seq_count, 2, HALF, 2, STATE),
         dt_part,
         a_log.reshape(1, heads),
         skip_scale.reshape(1, heads),

time: 115 us -> 111 us (0.965)
  local copies, waits for them, and re-layouts: 4.66 us -> 1.15 us
    reshape x1 -> x0, local copies, waits for them, and re-layouts: 1.99 us -> none  [mixer(): bc_part.reshape(seq_count, 2, HALF, 2 * STATE)]
    unnamed x1, local copies, waits for them, and re-layouts: 2.67 us -> 1.15 us
where the time goes in v6:
time: 111 us
  Pallas kernels  109 us (98%)
  local copies, waits for them, and re-layouts  1.15 us (1%)
    pallas_call x1, Pallas kernels, mix(): pl.pallas_call(mixer_kernel, out_shape=pltpu.VMEM((tokens, cols), low), i...  109 us

profile of v6, /device:TPU:1, one launch (start us, length us, event | category | flops | bytes accessed | tf_op | source)
XLA Modules:
  0.0 110.5 jit_solution(714466794229472742)
XLA Ops:
  0.0 109.3 %mixer.1 = bf16[768,1024]{1,0:T(8,128)(2,1)S(1)} custom-call(bf16[2,2,192,1024]{3,2,1,0:T(8,128)(2,1)} %bitcast.8, bf16[2,2,192,2,128]{4,3,2,1,0:T(2,128)(2,1)} %bitcast.10, f32[2,16,384]{2,1,0:T(8,128)} %dt_ref.1, f32[1,16]{1,0:T(1,128)} %bitcast.12, f32[1,16]{1,0:T(1,128)} %bitcast.13, f32[1,1024]{1,0:T(1,128)} %bitcast.11, f32[4,1024]{1,0:T(4,128)} %taps_ref.1, ...), custom_call_target="tpu_custom_call" | custom-call | tf_op jit(solution)/shard_map/mixer/pallas_call | solution.py:678
  109.4 1.1 %copy.12 = bf16[2,384,1024]{2,1,0:T(8,128)(2,1)} copy(bf16[2,384,1024]{2,1,0:T(8,128)(2,1)S(1)} %bitcast.7) | data formatting | bytes 3145728

commit v7 on v6

--- a/solution.py
+++ b/solution.py
@@ -56,10 +56,10 @@
 def mixer_kernel(
     x_ref, bc_ref, dt_ref, a_ref, skip_ref, gain_ref, taps_ref, taps_bc_ref, z_ref, w_ref,
     out_ref,
-    halo_x, halo_bc, wide, xs, bs, cs, cum_row, dt_row, cum_col, tail3, cum3, spread3, skips,
+    xbuf, halo_x, halo_bc, wide, xs, bs, cs, cum_row, dt_row, cum_col, tail3, cum3, spread3, skips,
     scaled, upd, sib, comp, got, back, came, give, ent, dec, dec_sib, dec_chip, decs, steps, pace,
     inner, zbuf, act, wts, mid, keep, direct, joined, own, relay, final,
-    z_sem, load_s, halo_s, halo_r, dec_s, dec_r, own_s, sib_s, sib_r, upd_s, upd_r, ent_s, ent_r,
+    x_sem, z_sem, load_s, halo_s, halo_r, dec_s, dec_r, own_s, sib_s, sib_r, upd_s, upd_r, ent_s, ent_r,
     give_s, give_r, in_s, in_r, side_s, side_r, near_s, near_r, far_s, far_r, core_s, core_r,
     y_s, y_r, mid_s, mid_r, fin_s, fin_r,
 ):
@@ -178,7 +178,7 @@
         rows = pl.ds(HALF - 16, 16)
         return (
             remote(
-                x_ref.at[:, half, rows], halo_x.at[half], halo_s.at[half, 0], halo_r.at[half, 0],
+                xbuf.at[:, half, rows], halo_x.at[half], halo_s.at[half, 0], halo_r.at[half, 0],
                 target,
             ),
             remote(
@@ -240,6 +240,8 @@
             back.at[chip, of_seq(s)], came.at[of_seq(s), share(chip)], own_s.at[s, 1]
         )
 
+    x_copy = pltpu.make_async_copy(x_ref, xbuf, x_sem)
+    x_copy.start()
     z_copy = pltpu.make_async_copy(z_ref, zbuf, z_sem)
     z_copy.start()
     barrier = pltpu.get_barrier_semaphore()
@@ -288,6 +290,7 @@
             tail3[b] = by_rows(eye, rounded_parts(tail)).astype(bf16)
             cum3[b] = by_rows(eye, rounded_parts(jnp.exp(cum))).astype(bf16)
     decays(0)
+    x_copy.wait()
     pl.semaphore_wait(barrier, 13)
     for half in range(2):
         for copy in halo(half):
@@ -363,9 +366,9 @@
             here = pl.ds(start, chunk)
             earlier = halo_x[0, s, :, here]
             earlier = jnp.where(me == 0, jnp.zeros_like(earlier), earlier)
-            turned = jnp.where(me == 15, x_ref[s, 0, HALF - 16 :, here], halo_x[1, s, :, here])
+            turned = jnp.where(me == 15, xbuf[s, 0, HALF - 16 :, here], halo_x[1, s, :, here])
             wide[0:8] = jnp.where(half == 0, earlier, turned).astype(f32)[8:]
-            wide[8:] = x_ref[s, half, :, here].astype(f32)
+            wide[8:] = xbuf[s, half, :, here].astype(f32)
             convolve(taps_ref[:, here], put)
             for r in range(0, HALF, band):
                 factor = jnp.dot(
@@ -678,9 +681,10 @@
     return pl.pallas_call(
         mixer_kernel,
         out_shape=pltpu.VMEM((tokens, cols), low),
-        in_specs=[vmem] * 8 + [hbm] * 2,
+        in_specs=[hbm] + [vmem] * 7 + [hbm] * 2,
         out_specs=vmem,
         scratch_shapes=[
+            pltpu.VMEM((2, 2, HALF, cols), low),
             pltpu.VMEM((2, 2, 16, cols), low),
             pltpu.VMEM((2, 2, 16, 2, STATE), low),
             pltpu.VMEM((8 + HALF, 256), wide),
@@ -720,7 +724,7 @@
             pltpu.VMEM((tokens, cols), wide),
             pltpu.VMEM((2, tokens, half), low),
             pltpu.VMEM((2, 2, tokens, half), low),
-            dma, dma((4,)), dma((2, 2)), dma((2, 2)), dma((8,)), dma((8,)), dma((2, 2)),
+            dma, dma, dma((4,)), dma((2, 2)), dma((2, 2)), dma((8,)), dma((8,)), dma((2, 2)),
             dma((2,)), dma((2,)), dma((2, 8)), dma((2, 8)), dma((2, 8)), dma((2, 8)),
             dma((2,)), dma((2,)), dma((4,)), dma((4,)), dma((4,)), dma((4,)),
             dma((4, 2, 2)), dma((4, 2, 2)), dma((4, 2)), dma((4, 2)), dma((4, 5)), dma((4, 5)),

time: 111 us -> 110 us (level)
  no operation moved by 1% of the time
where the time goes in v7:
time: 110 us
  Pallas kernels  109 us (99%)
  local copies, waits for them, and re-layouts  1.15 us (1%)
    pallas_call x1, Pallas kernels, mix(): pl.pallas_call(mixer_kernel, out_shape=pltpu.VMEM((tokens, cols), low), i...  109 us

profile of v7, /device:TPU:1, one launch (start us, length us, event | category | flops | bytes accessed | tf_op | source)
XLA Modules:
  0.0 110.0 jit_solution(15403017901486976863)
XLA Ops:
  0.0 108.8 %mixer.1 = bf16[768,1024]{1,0:T(8,128)(2,1)S(1)} custom-call(bf16[2,2,192,1024]{3,2,1,0:T(8,128)(2,1)} %bitcast.8, bf16[2,2,192,2,128]{4,3,2,1,0:T(2,128)(2,1)} %bitcast.10, f32[2,16,384]{2,1,0:T(8,128)} %dt_ref.1, f32[1,16]{1,0:T(1,128)} %bitcast.12, f32[1,16]{1,0:T(1,128)} %bitcast.13, f32[1,1024]{1,0:T(1,128)} %bitcast.11, f32[4,1024]{1,0:T(4,128)} %taps_ref.1, ...), custom_call_target="tpu_custom_call" | custom-call | tf_op jit(solution)/shard_map/mixer/pallas_call | solution.py:681
  108.8 1.1 %copy.12 = bf16[2,384,1024]{2,1,0:T(8,128)(2,1)} copy(bf16[2,384,1024]{2,1,0:T(8,128)(2,1)S(1)} %bitcast.7) | data formatting | bytes 3145728
